TPU v7x, 32 devices: a whole 2x2x4 slice. The times are simulated.
32 devices in a mesh: seq: 8 (over z, y), tp: 4 (over x, core).
Axes of the slice: x: 2, y: 2, z: 4, core: 2. Of those that a mesh axis runs over, the one named last changes fastest.
Arguments:
- tokens: bfloat16 [4096, 768], P('seq'), may hold values from -6 to 6
- cotangent: bfloat16 [4096, 768], P('seq'), may hold values from -6 to 6
- past_states: bfloat16 [4096, 768], P('seq'), may hold values from -6 to 6
- doc_ids: int32 [4096], P('seq'), may hold values from 0 to 4095, as said below
- cur_book: int32 [8], P('seq'), may hold values from 0 to 3
- past_book: int32 [8], P('seq'), may hold values from 0 to 3, as said below
- past_age: int32 [8], P('seq'), may hold values from 0 to 1, as said below
- ln1_gain: float32 [768], replicated, may hold values from 0.5 to 1.5
- ln1_bias: float32 [768], replicated, may hold values from -3 to 3
- qkv_weight: bfloat16 [768, 3, 768], P(None, None, 'tp'), may hold values from -0.21875 to 0.21875
- qv_bias: float32 [2, 768], P(None, 'tp'), may hold values from -3 to 3
- out_weight: bfloat16 [768, 768], P('tp'), may hold values from -0.75 to 0.75
- out_bias: float32 [768], replicated, may hold values from -3 to 3
- ln2_gain: float32 [768], replicated, may hold values from 0.5 to 1.5
- ln2_bias: float32 [768], replicated, may hold values from -3 to 3
- fc_weight: bfloat16 [768, 3072], P(None, 'tp'), may hold values from -0.21875 to 0.21875
- fc_bias: float32 [3072], P('tp'), may hold values from -3 to 3
- proj_weight: bfloat16 [3072, 768], P('tp'), may hold values from -0.109375 to 0.109375
- proj_bias: float32 [768], replicated, may hold values from -3 to 3
- mu_weight: float32 [12, 512], P('tp'), may hold values from -0.25 to 0.25
- sigma_weight: float32 [12, 512], P('tp'), may hold values from -0.25 to 0.25
Outputs:
- output: bfloat16 [4096, 768], P('seq')
- grad_tokens: bfloat16 [4096, 768], P('seq')
- grad_qkv_weight: float32 [768, 3, 768], P('seq', None, 'tp')
- grad_qv_bias: float32 [2, 768], P(None, 'tp')
- grad_out_weight: float32 [768, 768], P('tp', 'seq')
- grad_out_bias: float32 [768], replicated
- grad_fc_weight: float32 [768, 3072], P('seq', 'tp')
- grad_fc_bias: float32 [3072], P('tp')
- grad_proj_weight: float32 [3072, 768], P('tp', 'seq')
- grad_proj_bias: float32 [768], replicated
- grad_ln1_gain: float32 [768], replicated
- grad_ln1_bias: float32 [768], replicated
- grad_ln2_gain: float32 [768], replicated
- grad_ln2_bias: float32 [768], replicated
- grad_mu_weight: float32 [12, 512], P('tp')
- grad_sigma_weight: float32 [12, 512], P('tp')
Inputs may be any that keep to these rules, and one draw needn't show every extreme that they name: `doc_ids`: each token's value is the position of the last token of its document, so values never fall along the tokens. One document starts inside the first 512 tokens and ends inside the last 512; the others are short. `past_book`: each of the 4 books has exactly 2 past segments. `past_age`: within each book the ages of its past segments are 0 to 1, each once.
All inputs are finite; a program needn't handle non-finite values.
Results may differ from a plain program's by a relative error of at most 0.019.
Values may be sent and summed in bfloat16 or wider, within the bound.
A program may use at most 128 MiB of HBM per device.

v0:
```python
import math

import jax
import jax.numpy as jnp
from jax import lax
from jax.sharding import PartitionSpec as P

D = 768
DH = 64
NB = 512
SEG = 512
BOOKS = 4


EPS = 1e-05
TAU = 0.75
RIDGE = 1.0
SPREAD = 0.01
NEGATIVE = -1e30
UPPER_LIMIT = lax.Precision.HIGHEST


def shifted(block, axis, distance):
    devices = range(lax.axis_size(axis))
    route = [(i - distance, i) for i in devices if i - distance in devices]
    return lax.ppermute(block, axis, route)


def passed_along(block, axis, distance):
    devices = range(lax.axis_size(axis))
    route = [((i - distance) % len(devices), i) for i in devices]
    return lax.ppermute(block, axis, route)


def layer_norm(rows_in, gain_vec, bias_vec):
    average = jnp.mean(rows_in, axis=-1, keepdims=True)
    centred = rows_in - average
    variance = jnp.mean(centred * centred, axis=-1, keepdims=True)
    return centred * lax.rsqrt(variance + EPS) * gain_vec + bias_vec


def gelu_tanh(pre_act):
    return jax.nn.gelu(pre_act, approximate=True)


def radial_centres(basis_n):
    return (jnp.arange(basis_n, dtype=jnp.float32) + 0.5) / basis_n


def past_basis(seg_ages, basis_n, seg_len):
    shrink = jnp.power(jnp.float32(TAU), seg_ages.astype(jnp.float32))
    inside = (jnp.arange(seg_len, dtype=jnp.float32) + 0.5) / seg_len
    time_pts = shrink[:, None] * (TAU + (1.0 - TAU) * inside[None, :])
    offset = (time_pts[:, None, :] - radial_centres(basis_n)[None, :, None]) * basis_n
    return jnp.exp(-0.5 * offset * offset)


def memory_density(affinity, mu_weight, sigma_weight):
    basis_n = mu_weight.shape[1]
    rbf_width = 1.0 / basis_n
    centre = jax.nn.sigmoid(
        jnp.einsum("...hn,hn->...h", affinity, mu_weight, precision=UPPER_LIMIT)
    )
    unconstrained_spread = jnp.einsum(
        "...hn,hn->...h", affinity, sigma_weight, precision=UPPER_LIMIT
    )
    spread_sq = SPREAD * jax.nn.softplus(unconstrained_spread) + rbf_width * rbf_width
    centre_gap = centre[..., None] - radial_centres(basis_n)
    return (
        rbf_width
        * lax.rsqrt(spread_sq)[..., None]
        * jnp.exp(-0.5 * centre_gap * centre_gap / spread_sq[..., None])
    )


def shared_solver(factor):

    def solve_all(rhs_books):

        def solve_one(rhs_mat):
            return jax.scipy.linalg.cho_solve((factor, True), rhs_mat)

        return jax.vmap(solve_one)(rhs_books)

    return solve_all


def block_rows(row_count_total, tok_rows):
    return math.gcd(row_count_total, max(512, tok_rows))


def split_blocks(array_in, blk_rows):
    blk_count = array_in.shape[0] // blk_rows
    return array_in.reshape((blk_count, blk_rows) + array_in.shape[1:])


def keep_state(running):
    return running


def forward_folder(queries, own_pos, own_doc, scale_dh, fold_state, shard_piece):
    key_part, val_part, doc_part = shard_piece
    blk_rows = block_rows(key_part.shape[0], queries.shape[0])
    blk_count = key_part.shape[0] // blk_rows

    def one_block(running, block_item):
        key_blk, val_blk, doc_blk, blk_index = block_item
        key_pos = blk_index * blk_rows + jnp.arange(blk_rows, dtype=jnp.int32)

        def one_compute(current):
            row_max, row_sum, accumulated = current
            visible = (
                (own_pos[:, None] >= key_pos[None, :]) & (own_doc[:, None] == doc_blk[None, :])
            )[:, None, :]
            scores = (
                jnp.einsum("qhd,khd->qhk", queries, key_blk, preferred_element_type=jnp.float32)
                * scale_dh
            )
            scores = jnp.where(visible, scores, NEGATIVE)
            new_max = jnp.maximum(row_max, jnp.max(scores, axis=-1))
            exp_vals = jnp.where(visible, jnp.exp(scores - new_max[..., None]), 0.0)
            adjustment_term = jnp.exp(row_max - new_max)
            new_sum = row_sum * adjustment_term + jnp.sum(exp_vals, axis=-1)
            new_acc = accumulated * adjustment_term[..., None] + jnp.einsum(
                "qhk,khd->qhd",
                exp_vals.astype(jnp.bfloat16),
                val_blk,
                preferred_element_type=jnp.float32,
            )
            return (new_max, new_sum, new_acc)

        return (lax.cond(key_pos[0] <= own_pos[-1], one_compute, keep_state, running), None)

    blocks = (
        split_blocks(key_part, blk_rows),
        split_blocks(val_part, blk_rows),
        split_blocks(doc_part, blk_rows),
        jnp.arange(blk_count, dtype=jnp.int32),
    )
    result, unused = lax.scan(one_block, fold_state, blocks)
    return result


def local(
    tokens,
    cotangent,
    past_states,
    doc_ids,
    cur_book,
    past_book,
    past_age,
    ln1_gain,
    ln1_bias,
    qkv_weight,
    qv_bias,
    out_weight,
    out_bias,
    ln2_gain,
    ln2_bias,
    fc_weight,
    fc_bias,
    proj_weight,
    proj_bias,
    mu_weight,
    sigma_weight,
):
    tok_rows = tokens.shape[0]
    heads_here = mu_weight.shape[0]
    head_cols = qkv_weight.shape[2]
    seg_here = cur_book.shape[0]
    seq_count = lax.axis_size("seq")
    seq_index = lax.axis_index("seq")
    scale_dh = DH ** (-0.5)
    head_shape = (tok_rows, heads_here, DH)
    own_pos = seq_index * tok_rows + jnp.arange(tok_rows, dtype=jnp.int32)
    book_ids = jnp.arange(BOOKS, dtype=jnp.int32)
    past_member = (past_book[:, None] == book_ids[None, :]).astype(jnp.float32)
    read_member = (cur_book[:, None] == book_ids[None, :]).astype(jnp.bfloat16)
    all_ages = jnp.arange(seq_count * seg_here // BOOKS, dtype=jnp.int32)
    basis_of_ages = past_basis(all_ages, NB, SEG)
    book_gram_matrix = jnp.einsum(
        "fgx,fhx->gh", basis_of_ages, basis_of_ages, precision=UPPER_LIMIT
    )
    factor = jnp.linalg.cholesky(book_gram_matrix + RIDGE * jnp.eye(NB, dtype=jnp.float32))
    solve_all = shared_solver(factor)
    past_rows = past_states.reshape(seg_here, SEG, D).astype(jnp.float32)
    basis_vals = past_basis(past_age, NB, SEG)
    proj_seg = jnp.einsum("snt,std->snd", basis_vals, past_rows, precision=UPPER_LIMIT)
    kv_weight = qkv_weight[:, 1:].astype(jnp.float32).reshape(D, 2 * head_cols)
    proj_sum = lax.psum(
        jnp.einsum("sb,snd->bnd", past_member, proj_seg, precision=UPPER_LIMIT), "seq"
    )
    coeffs = solve_all(proj_sum)
    mem_kv = jnp.einsum("bnd,dm->bnm", coeffs, kv_weight, precision=UPPER_LIMIT)
    mem_seg = jnp.einsum(
        "sb,bnm->snm", read_member, mem_kv.astype(jnp.bfloat16), preferred_element_type=jnp.float32
    ).astype(jnp.bfloat16)
    mem_keys = mem_seg[:, :, :head_cols].reshape(seg_here, NB, heads_here, DH)
    mem_vals = mem_seg[:, :, head_cols:].reshape(seg_here, NB, heads_here, DH)
    hidden_in = tokens.astype(jnp.float32)
    normed_one_f, norm_one_back = jax.vjp(layer_norm, hidden_in, ln1_gain, ln1_bias)
    normed_one = normed_one_f.astype(jnp.bfloat16)
    mixed_qkv = jnp.einsum(
        "td,dcm->tcm", normed_one, qkv_weight, preferred_element_type=jnp.float32
    )
    queries = (mixed_qkv[:, 0] + qv_bias[0]).astype(jnp.bfloat16).reshape(head_shape)
    key_rows = mixed_qkv[:, 1].astype(jnp.bfloat16).reshape(head_shape)
    val_rows = (mixed_qkv[:, 2] + qv_bias[1]).astype(jnp.bfloat16).reshape(head_shape)
    zero_heads = jnp.zeros(head_shape, jnp.float32)
    fold_init = (
        jnp.full((tok_rows, heads_here), NEGATIVE, jnp.float32),
        jnp.zeros((tok_rows, heads_here), jnp.float32),
        zero_heads,
    )
    row_max, row_sum, accumulated = forward_folder(
        queries,
        own_pos,
        doc_ids,
        scale_dh,
        fold_init,
        (
            lax.all_gather(key_rows, "seq", axis=0, tiled=True),
            lax.all_gather(val_rows, "seq", axis=0, tiled=True),
            lax.all_gather(doc_ids, "seq", axis=0, tiled=True),
        ),
    )
    log_sum = row_max + jnp.log(row_sum)
    local_out = accumulated / row_sum[..., None]
    seg_queries = queries.reshape(seg_here, SEG, heads_here, DH)
    affinity = (
        jnp.einsum("sthd,snhd->sthn", seg_queries, mem_keys, preferred_element_type=jnp.float32)
        * scale_dh
    )
    density, density_back = jax.vjp(memory_density, affinity, mu_weight, sigma_weight)
    density_bf = density.astype(jnp.bfloat16)
    mem_out = jnp.einsum(
        "sthn,snhd->sthd", density_bf, mem_vals, preferred_element_type=jnp.float32
    ).reshape(head_shape)
    heads_out = (local_out + mem_out).astype(jnp.bfloat16).reshape(tok_rows, head_cols)
    branch_one = (
        lax.psum(
            jnp.dot(heads_out, out_weight, preferred_element_type=jnp.float32).astype(jnp.bfloat16),
            "tp",
        ).astype(jnp.float32)
        + out_bias
    )
    residual = hidden_in + branch_one
    normed_two_f, norm_two_back = jax.vjp(layer_norm, residual, ln2_gain, ln2_bias)
    normed_two = normed_two_f.astype(jnp.bfloat16)
    pre_act = jnp.dot(normed_two, fc_weight, preferred_element_type=jnp.float32) + fc_bias
    activated, gelu_back = jax.vjp(gelu_tanh, pre_act)
    act_bf = activated.astype(jnp.bfloat16)
    branch_two = (
        lax.psum(
            jnp.dot(act_bf, proj_weight, preferred_element_type=jnp.float32).astype(jnp.bfloat16),
            "tp",
        ).astype(jnp.float32)
        + proj_bias
    )
    output = (residual + branch_two).astype(jnp.bfloat16)
    grad_out = cotangent.astype(jnp.float32)
    grad_proj_w = jnp.einsum("tf,td->fd", act_bf, cotangent, preferred_element_type=jnp.float32)
    grad_proj_b = jnp.sum(grad_out, axis=0)
    (grad_pre,) = gelu_back(
        jnp.einsum("td,fd->tf", cotangent, proj_weight, preferred_element_type=jnp.float32)
    )
    pre_bf = grad_pre.astype(jnp.bfloat16)
    grad_fc_w = jnp.einsum("td,tf->df", normed_two, pre_bf, preferred_element_type=jnp.float32)
    grad_fc_b = jnp.sum(pre_bf.astype(jnp.float32), axis=0)
    grad_normed_two = lax.psum(
        jnp.einsum("tf,df->td", pre_bf, fc_weight, preferred_element_type=jnp.float32).astype(
            jnp.bfloat16
        ),
        "tp",
    ).astype(jnp.float32)
    grad_resid_part, grad_ln2_g, grad_ln2_b = norm_two_back(grad_normed_two)
    grad_resid = grad_out + grad_resid_part
    resid_bf = grad_resid.astype(jnp.bfloat16)
    grad_out_w = jnp.einsum("tm,td->md", heads_out, resid_bf, preferred_element_type=jnp.float32)
    grad_out_b = jnp.sum(resid_bf.astype(jnp.float32), axis=0)
    grad_heads = (
        jnp.einsum("td,md->tm", resid_bf, out_weight, preferred_element_type=jnp.float32)
        .astype(jnp.bfloat16)
        .reshape(head_shape)
    )
    seg_grad = grad_heads.reshape(seg_here, SEG, heads_here, DH)
    grad_density = jnp.einsum(
        "sthd,snhd->sthn", seg_grad, mem_vals, preferred_element_type=jnp.float32
    )
    grad_mem_vals = jnp.einsum(
        "sthn,sthd->snhd", density_bf, seg_grad, preferred_element_type=jnp.float32
    )
    grad_aff, grad_mu_w, grad_sigma_w = density_back(grad_density)
    aff_bf = grad_aff.astype(jnp.bfloat16)
    grad_q_mem = (
        jnp.einsum("sthn,snhd->sthd", aff_bf, mem_keys, preferred_element_type=jnp.float32).reshape(
            head_shape
        )
        * scale_dh
    )
    grad_mem_keys = (
        jnp.einsum("sthn,sthd->snhd", aff_bf, seg_queries, preferred_element_type=jnp.float32)
        * scale_dh
    )
    grad_mem_seg = jnp.concatenate(
        [
            grad_mem_keys.reshape(seg_here, NB, head_cols),
            grad_mem_vals.reshape(seg_here, NB, head_cols),
        ],
        axis=-1,
    )
    grad_mem_books = jnp.einsum(
        "sb,snm->bnm", read_member.astype(jnp.float32), grad_mem_seg, precision=UPPER_LIMIT
    )
    row_delta = jnp.sum(grad_heads.astype(jnp.float32) * local_out, axis=-1)

    def cycle_step(step, carry):
        key_blk, val_blk, doc_blk, grad_k, grad_v, grad_q = carry
        anchor = (seq_index - step) % seq_count
        key_pos = anchor * tok_rows + jnp.arange(tok_rows, dtype=jnp.int32)

        def cycle_compute(current):
            acc_k, acc_v, acc_q = current
            visible = (
                (own_pos[:, None] >= key_pos[None, :]) & (doc_ids[:, None] == doc_blk[None, :])
            )[:, None, :]
            scores = (
                jnp.einsum("qhd,khd->qhk", queries, key_blk, preferred_element_type=jnp.float32)
                * scale_dh
            )
            prob_vals = jnp.where(
                visible, jnp.exp(jnp.where(visible, scores, NEGATIVE) - log_sum[..., None]), 0.0
            )
            acc_v = acc_v + jnp.einsum(
                "qhk,qhd->khd",
                prob_vals.astype(jnp.bfloat16),
                grad_heads,
                preferred_element_type=jnp.float32,
            )
            grad_prob = jnp.einsum(
                "qhd,khd->qhk", grad_heads, val_blk, preferred_element_type=jnp.float32
            )
            grad_score = (prob_vals * (grad_prob - row_delta[..., None])).astype(jnp.bfloat16)
            acc_q = (
                acc_q
                + jnp.einsum(
                    "qhk,khd->qhd", grad_score, key_blk, preferred_element_type=jnp.float32
                )
                * scale_dh
            )
            acc_k = (
                acc_k
                + jnp.einsum(
                    "qhk,qhd->khd", grad_score, queries, preferred_element_type=jnp.float32
                )
                * scale_dh
            )
            return (acc_k, acc_v, acc_q)

        grad_k, grad_v, grad_q = lax.cond(
            anchor <= seq_index, cycle_compute, keep_state, (grad_k, grad_v, grad_q)
        )
        key_blk, val_blk, doc_blk = shifted((key_blk, val_blk, doc_blk), "seq", 1)
        grad_k, grad_v = (
            passed_along(grad_k.astype(jnp.bfloat16), "seq", 1).astype(grad_k.dtype),
            passed_along(grad_v.astype(jnp.bfloat16), "seq", 1).astype(grad_v.dtype),
        )
        return (key_blk, val_blk, doc_blk, grad_k, grad_v, grad_q)

    cycle_init = (key_rows, val_rows, doc_ids, zero_heads, zero_heads, zero_heads)
    cycle_final = lax.fori_loop(0, seq_count, cycle_step, cycle_init)
    grad_keys, grad_vals, grad_q_local = (cycle_final[3], cycle_final[4], cycle_final[5])
    grad_q_bf = (grad_q_local + grad_q_mem).astype(jnp.bfloat16).reshape(tok_rows, head_cols)
    grad_k_bf = grad_keys.astype(jnp.bfloat16).reshape(tok_rows, head_cols)
    grad_v_bf = grad_vals.astype(jnp.bfloat16).reshape(tok_rows, head_cols)
    grad_qkv = jnp.stack([grad_q_bf, grad_k_bf, grad_v_bf], axis=1)
    grad_qkv_w = jnp.einsum("td,tcm->dcm", normed_one, grad_qkv, preferred_element_type=jnp.float32)
    grad_kv_w = jnp.einsum("bnd,bnm->dm", coeffs, grad_mem_books, precision=UPPER_LIMIT)
    grad_qkv_w = grad_qkv_w.at[:, 1:].add(grad_kv_w.reshape(D, 2, head_cols))
    grad_qv_b = jnp.stack(
        [
            jnp.sum(grad_q_bf.astype(jnp.float32), axis=0),
            jnp.sum(grad_v_bf.astype(jnp.float32), axis=0),
        ]
    )
    grad_normed_one = lax.psum(
        jnp.einsum("tcm,dcm->td", grad_qkv, qkv_weight, preferred_element_type=jnp.float32).astype(
            jnp.bfloat16
        ),
        "tp",
    ).astype(jnp.float32)
    grad_in_part, grad_ln1_g, grad_ln1_b = norm_one_back(grad_normed_one)
    grad_tokens = (grad_resid + grad_in_part).astype(jnp.bfloat16)
    qkv_share, out_share, fc_share, proj_share = (
        lax.psum_scatter(grad_qkv_w, "seq", scatter_dimension=0, tiled=True),
        lax.psum_scatter(grad_out_w, "seq", scatter_dimension=1, tiled=True),
        lax.psum_scatter(grad_fc_w, "seq", scatter_dimension=0, tiled=True),
        lax.psum_scatter(grad_proj_w, "seq", scatter_dimension=1, tiled=True),
    )
    small_sums = lax.psum(
        (
            grad_ln1_g,
            grad_ln1_b,
            grad_qv_b,
            grad_out_b,
            grad_ln2_g,
            grad_ln2_b,
            grad_fc_b,
            grad_proj_b,
            grad_mu_w,
            grad_sigma_w,
        ),
        "seq",
    )
    return (
        output,
        grad_tokens,
        qkv_share,
        small_sums[2],
        out_share,
        small_sums[3],
        fc_share,
        small_sums[6],
        proj_share,
        small_sums[7],
        small_sums[0],
        small_sums[1],
        small_sums[4],
        small_sums[5],
        small_sums[8],
        small_sums[9],
    )


def solution(mesh):
    in_specs = (
        P("seq", None),
        P("seq", None),
        P("seq", None),
        P("seq"),
        P("seq"),
        P("seq"),
        P("seq"),
        P(),
        P(),
        P(None, None, "tp"),
        P(None, "tp"),
        P("tp", None),
        P(),
        P(),
        P(),
        P(None, "tp"),
        P("tp"),
        P("tp", None),
        P(),
        P("tp", None),
        P("tp", None),
    )
    out_specs = (
        P("seq", None),
        P("seq", None),
        P("seq", None, "tp"),
        P(None, "tp"),
        P("tp", "seq"),
        P(),
        P("seq", "tp"),
        P("tp"),
        P("tp", "seq"),
        P(),
        P(),
        P(),
        P(),
        P(),
        P("tp", None),
        P("tp", None),
    )
    return jax.shard_map(local, mesh=mesh, in_specs=in_specs, out_specs=out_specs, check_vma=False)
```

profile of v0, /device:TPU:0, one launch (start us, length us, event | category | flops | bytes accessed | tf_op | source)
XLA Modules:
  0.0 1081.1 jit_solution(12815203642947959632)
XLA Ops:
  21.0 3.8 multiply_bitcast_fusion
  26.9 4.3 fusion.155
  35.1 11.7 %cholesky.104 = f32[128,128]{1,0:T(8,128)S(1)} custom-call(f32[128,128]{1,0:T(8,128)S(1)} %cholesky.266), custom_call_target="Cholesky" | custom-call | tf_op jit(solution)/shard_map/jit(cholesky)/cholesky | solution.py:184
  46.8 9.8 custom-call.34
  60.0 12.1 %cholesky.217 = f32[128,128]{1,0:T(8,128)S(1)} custom-call(f32[128,128]{1,0:T(8,128)S(1)} %cholesky.270), custom_call_target="Cholesky" | custom-call | tf_op jit(solution)/shard_map/jit(cholesky)/cholesky | solution.py:184
  72.1 9.8 custom-call.35
  85.0 13.2 %cholesky.238 = f32[128,128]{1,0:T(8,128)} custom-call(f32[128,128]{1,0:T(8,128)} %cholesky.275), custom_call_target="Cholesky" | custom-call | tf_op jit(solution)/shard_map/jit(cholesky)/cholesky | solution.py:184
  100.2 11.3 %custom-call.36 = f32[1,128,128]{1,2,0:T(8,128)} custom-call(f32[1,128,128]{2,1,0:T(8,128)} %get-tuple-element.900), custom_call_target="InvertDiagBlocksLowerTriangular" | custom-call | tf_op jit(solution)/shard_map/jit(cholesky)/cholesky | solution.py:184
  113.8 11.9 %cholesky.255 = f32[128,128]{1,0:T(8,128)S(1)} custom-call(f32[128,128]{1,0:T(8,128)S(1)} %convolution_subtract_fusion.6), custom_call_target="Cholesky" | custom-call | tf_op jit(solution)/shard_map/jit(cholesky)/cholesky | solution.py:184
  132.6 14.0 %while.43 = (s32[]{:T(128)}, f32[512,512]{1,0:T(8,128)}, s32[4,2]{0,1:T(2,128)S(1)}, f32[4,128,128]{2,1,0:T(8,128)}, s32[]{:T(128)}) while((s32[]{:T(128)}, f32[512,512]{1,0:T(8,128)}, s32[4,2]{0,1:T(2,128)S(1)}, f32[4,128,128]{2,1,0:T(8,128)}, s32[]{:T(128)}) %tuple.157), condition=%wide.while_cond.1, body=%wide.while_body.1.sunk | while | flops 2 | bytes 132705 | solution.py:81
  146.6 40.8 %custom-call.37 = f32[4,128,128]{1,2,0:T(8,128)} custom-call(f32[4,128,128]{2,1,0:T(8,128)} %get-tuple-element.624), custom_call_target="InvertDiagBlocksLowerTriangular" | custom-call | tf_op jit(solution)/shard_map/vmap(jit(_cho_solve))/triangular_solve | solution.py:81
  188.1 28.5 %all-gather = s32[8,1,512]{2,1,0:T(1,128)S(1)} all-gather(s32[1,1,512]{2,1,0:T(1,128)S(1)} %bitcast.443), channel_id=1, replica_groups=mesh['seq'=8,'tp'=4] {'seq'}, dimensions={0}, use_global_device_ids=true | all-gather | bytes 18432 | tf_op jit(solution)/shard_map/all_gather | solution.py:224
  224.4 47.6 %while.42 = (s32[]{:T(128)}, f32[512,3]{0,1:T(4,128)S(1)}, f32[512,3]{0,1:T(4,128)S(1)}, f32[512,3,64]{0,2,1:T(8,128)}, s32[8]{0:T(128)}, /*index=5*/s32[512]{0:...) while((s32[]{:T(128)}, f32[512,3]{0,1:T(4,128)S(1)}, ...), condition=%wide.region_7.8_spmd, body=%wide.region_2.7_spmd.sunk | while | flops 212536832 | bytes 15129507 | solution.py:140
  229.4 7.2 conditional.5
  272.0 51.2 %all-reduce.8.cloned.1.call-done = f32[512,768,4]{0,2,1:T(4,128)} async-done(((f32[512,768,4]{0,2,1:T(4,128)}), f32[512,768,4]{0,2,1:T(4,128)}) %all-reduce.8.cloned.1.call-update) | async-done | bytes 6291472 | tf_op jit(solution)/shard_map/psum | solution.py:190
  323.2 5.2 fusion.282
  341.9 3.8 convolution_subtract_fusion.3
  352.3 5.8 fusion.68
  369.1 3.9 fusion.65
  377.6 6.6 copy.83
  384.1 7.5 reshape.639
  391.7 7.7 copy.84
  399.4 7.1 fusion.113
  423.9 27.6 %all-reduce.10.cloned.1.call-done = bf16[512,768]{1,0:T(8,128)(2,1)} async-done(((bf16[512,768]{1,0:T(8,128)(2,1)}), bf16[512,768]{1,0:T(8,128)(2,1)}) %all-reduce.10.cloned.1.call-update) | async-done | bytes 786448 | tf_op jit(solution)/shard_map/psum | solution.py:241
  461.9 3.7 convolution_convert_fusion.1
  465.6 30.3 %all-reduce.12.cloned.1.call-done = bf16[512,768]{1,0:T(8,128)(2,1)} async-done(((bf16[512,768]{1,0:T(8,128)(2,1)}), bf16[512,768]{1,0:T(8,128)(2,1)}) %all-reduce.12.cloned.1.call-update) | async-done | bytes 786448 | tf_op jit(solution)/shard_map/psum | solution.py:270
  507.5 230.9 %while.44 = (s32[]{:T(128)}, bf16[512,3,64]{0,2,1:T(8,128)(2,1)S(1)}, bf16[512,3,64]{0,2,1:T(8,128)(2,1)S(1)}, s32[512]{0:T(512)S(1)}, f32[512,3,64]{0,2,1:T(8,1...) while((s32[]{:T(128)}, ...), condition=%wide.region_28.29_spmd.clone, body=%wide.region_25.28_spmd.clone.sunk | while | flops 514622464 | bytes 28189460 | solution.py:371
  509.8 10.9 %conditional.6 = ((f32[512,3,64]{0,2,1:T(8,128)S(1)}, f32[512,3,64]{0,2,1:T(8,128)}, f32[512,3,64]{0,2,1:T(8,128)})) conditional(s32[]{:T(128)} %convert_element_type.481, (f32[512,3,64]{0,2,1:T(8,128)S(1)}, f32[512,3,64]{0,2,1:T(8,128)}, f32[512,3,64]{0,2,1:T(8,128)}) %tuple.151, (s32[]{:T(128)}, s32[]{:T(128)}, s32[512]{0:T(512)S(1)}, ...), branch_computations={%region_26.26_spmd, %region_27.27_spmd} | conditional | flops 514032640 | bytes 20310152 | solution.py:360
  540.5 13.3 %collective-permute-start.3 = (bf16[512,3,64]{0,2,1:T(8,128)(2,1)S(1)}, bf16[512,3,64]{0,2,1:T(8,128)(2,1)S(1)}, u32[]{:S(2)}, u32[]{:S(2)}) collective-permute-start(bf16[512,3,64]{0,2,1:T(8,128)(2,1)S(1)} %convert_element_type.482), channel_id=1, source_target_pairs={{28,0},{0,4},{4,8},{8,12},{12,16},{16,20},{20,24},{24,28},{29,1},{... | collective-permute-start | bytes 589832 | tf_op jit(solution)/shard_map/while/body/eval_jaxpr/ppermute | solution.py:32
  559.8 4.3 collective-permute-start.1
  575.5 13.5 %collective-permute-start.4 = (bf16[512,3,64]{0,2,1:T(8,128)(2,1)S(1)}, bf16[512,3,64]{0,2,1:T(8,128)(2,1)S(1)}, u32[]{:S(2)}, u32[]{:S(2)}) collective-permute-start(bf16[512,3,64]{0,2,1:T(8,128)(2,1)S(1)} %convert_element_type.484), channel_id=1, source_target_pairs={{28,0},{0,4},{4,8},{8,12},{12,16},{16,20},{20,24},{24,28},{29,1},{... | collective-permute-start | bytes 589832 | tf_op jit(solution)/shard_map/while/body/eval_jaxpr/ppermute | solution.py:32
  591.3 4.5 collective-permute-start.1
  609.0 13.4 %collective-permute-start = (bf16[512,3,64]{0,2,1:T(8,128)(2,1)}, bf16[512,3,64]{0,2,1:T(8,128)(2,1)S(1)}, u32[]{:S(2)}, u32[]{:S(2)}) collective-permute-start(bf16[512,3,64]{0,2,1:T(8,128)(2,1)} %copy.212), channel_id=1, source_target_pairs={{0,4},{4,8},{8,12},{12,16},{16,20},{20,24},{24,28},{1,5},{5,9},{9,... | collective-permute-start | bytes 589832 | tf_op jit(solution)/shard_map/while/body/eval_jaxpr/ppermute | solution.py:26
  622.5 4.2 collective-permute-start.1
  642.5 15.0 %collective-permute-start.1 = (bf16[512,3,64]{0,2,1:T(8,128)(2,1)}, bf16[512,3,64]{0,2,1:T(8,128)(2,1)S(1)}, u32[]{:S(2)}, u32[]{:S(2)}) collective-permute-start(bf16[512,3,64]{0,2,1:T(8,128)(2,1)} %copy.213), channel_id=1, source_target_pairs={{0,4},{4,8},{8,12},{12,16},{16,20},{20,24},{24,28},{1,5},{5,9},{9,... | collective-permute-start | bytes 589832 | tf_op jit(solution)/shard_map/while/body/eval_jaxpr/ppermute | solution.py:26
  671.2 5.2 collective-permute-start.1
  676.4 12.5 %collective-permute-start.2 = (s32[512]{0:T(512)S(1)}, s32[512]{0:T(512)S(1)}, u32[]{:S(2)}, u32[]{:S(2)}) collective-permute-start(s32[512]{0:T(512)S(1)} %copy.214), channel_id=1, source_target_pairs={{0,4},{4,8},{8,12},{12,16},{16,20},{20,24},{24,28},{1,5},{5,9},{9,... | collective-permute-start | bytes 6152 | tf_op jit(solution)/shard_map/while/body/eval_jaxpr/ppermute | solution.py:26
  703.0 3.8 collective-permute-start.2
  713.0 9.3 collective-permute-start.3
  750.0 12.4 %fusion.46 = f32[768,384,1]{0,1,2:T(8,128)S(1)} fusion(f32[512,768,4]{1,0,2:T(8,128)} %copy.84, f32[512,384]{0,1:T(8,128)S(1)} %maximum_bitcast_fusion, f32[4]{0:T(128)S(1)} %copy-done.106), kind=kOutput, calls=%fused_computation.54 | convolution fusion | flops 7248543744 | bytes 8257552 | tf_op jit(solution)/shard_map/bnd,bnm->dm/dot_general | solution.py:378
  768.7 4.3 fusion.275
  778.3 15.6 %all-reduce.14.cloned.1.call-done = (bf16[512,768]{1,0:T(8,128)(2,1)}, bf16[512,768]{1,0:T(8,128)(2,1)}) async-done(((bf16[512,768]{1,0:T(8,128)(2,1)}, bf16[512,768]{1,0:T(8,128)(2,1)}), (bf16[512,768]{1,0:T(8,128)(2,1)}, bf16[512,768]{1,0:T(8,128)(2,1)})) %all-reduce.14.cloned.1.call-update) | async-done | bytes 1572880 | tf_op jit(solution)/shard_map/psum | solution.py:254
  797.1 3.8 add_convert_fusion.1
  800.9 38.4 %all-reduce.1 = (f32[2,192]{1,0:T(2,128)}, f32[768]{0:T(1024)}, f32[768]{0:T(1024)}, f32[768]{0:T(1024)}, f32[768]{0:T(1024)}, /*index=5*/f32[768]{0:T(1024)}, f...) all-reduce(f32[2,192]{1,0:T(2,128)S(1)} %pad_maximum_fusion.2, ...), channel_id=1, replica_groups=mesh['seq'=8,'tp'=4] {'seq'}, use_global_device_ids=true, to_apply=%region_38.39 | all-reduce | flops 8832 | bytes 70656 | tf_op jit(solution)/shard_map/psum | solution.py:400
  839.3 20.8 %reduce-scatter.15.cloned.1.call-done = f32[96,192]{1,0:T(8,128)} async-done(((f32[768,192]{1,0:T(8,128)}), f32[96,192]{1,0:T(8,128)}) %reduce-scatter.15.cloned.1.call-update) | async-done | bytes 73744
  861.8 67.5 %reduce-scatter.13.cloned.1.call-done = f32[96,576]{1,0:T(8,128)} async-done(((f32[768,576]{1,0:T(8,128)}), f32[96,576]{1,0:T(8,128)}) %reduce-scatter.13.cloned.1.call-update) | async-done | bytes 221200
  931.3 70.4 %reduce-scatter.9.cloned.1.call-done = f32[96,768]{1,0:T(8,128)} async-done(((f32[768,768]{1,0:T(8,128)}), f32[96,768]{1,0:T(8,128)}) %reduce-scatter.9.cloned.1.call-update) | async-done | bytes 294928 | tf_op jit(solution)/shard_map/reduce_scatter | solution.py:397
  1001.6 72.4 %reduce-scatter.11.cloned.1.call-done = f32[768,96]{0,1:T(8,128)} async-done(((f32[768,768]{0,1:T(8,128)}), f32[768,96]{0,1:T(8,128)}) %reduce-scatter.11.cloned.1.call-update) | async-done | bytes 294928 | tf_op jit(solution)/shard_map/reduce_scatter | solution.py:398
  (584 shorter events, 321.5 us)
Async XLA Ops:
  7.2 211.4 %all-gather.6.cloned.1.call-start = ((), (), s32[]{:S(2)}) async-start(), calls=%async_computation.5 | async-start | bytes 1769472 | tf_op jit(solution)/shard_map/all_gather | solution.py:223
  14.9 206.5 %all-gather.4.cloned.1.call-start = ((), (), s32[]{:S(2)}) async-start(), calls=%async_computation.4 | async-start | bytes 1769472 | tf_op jit(solution)/shard_map/all_gather | solution.py:222
  16.7 306.5 %all-reduce.8.cloned.1.call-start = ((), (), s32[]{:S(2)}) async-start(), calls=%async_computation.6 | async-start | bytes 12582912 | tf_op jit(solution)/shard_map/psum | solution.py:190
  24.9 426.6 %all-reduce.10.cloned.1.call-start = ((), (), s32[]{:S(2)}) async-start(), calls=%async_computation.7 | async-start | bytes 1572864 | tf_op jit(solution)/shard_map/psum | solution.py:241
  417.7 78.3 %all-reduce.12.cloned.1.call-start = ((), (), s32[]{:S(2)}) async-start(), calls=%async_computation.8 | async-start | bytes 1572864 | tf_op jit(solution)/shard_map/psum | solution.py:270
  461.1 332.7 %all-reduce.14.cloned.1.call-start = ((), (), s32[]{:S(2)}) async-start(), calls=%async_computation.13 | async-start | bytes 3145728 | tf_op jit(solution)/shard_map/psum | solution.py:254
  520.7 14.2 %collective-permute-start.3 = (bf16[512,3,64]{0,2,1:T(8,128)(2,1)S(1)}, bf16[512,3,64]{0,2,1:T(8,128)(2,1)S(1)}, u32[]{:S(2)}, u32[]{:S(2)}) collective-permute-start(bf16[512,3,64]{0,2,1:T(8,128)(2,1)S(1)} %convert_element_type.482), channel_id=1, source_target_pairs={{28,0},{0,4},{4,8},{8,12},{12,16},{16,20},{20,24},{24,28},{29,1},{... | collective-permute-start | bytes 589832 | tf_op jit(solution)/shard_map/while/body/eval_jaxpr/ppermute | solution.py:32
  523.2 11.7 %collective-permute-start.4 = (bf16[512,3,64]{0,2,1:T(8,128)(2,1)S(1)}, bf16[512,3,64]{0,2,1:T(8,128)(2,1)S(1)}, u32[]{:S(2)}, u32[]{:S(2)}) collective-permute-start(bf16[512,3,64]{0,2,1:T(8,128)(2,1)S(1)} %convert_element_type.484), channel_id=1, source_target_pairs={{28,0},{0,4},{4,8},{8,12},{12,16},{16,20},{20,24},{24,28},{29,1},{... | collective-permute-start | bytes 589832 | tf_op jit(solution)/shard_map/while/body/eval_jaxpr/ppermute | solution.py:32
  524.8 13.5 %collective-permute-start = (bf16[512,3,64]{0,2,1:T(8,128)(2,1)}, bf16[512,3,64]{0,2,1:T(8,128)(2,1)S(1)}, u32[]{:S(2)}, u32[]{:S(2)}) collective-permute-start(bf16[512,3,64]{0,2,1:T(8,128)(2,1)} %copy.212), channel_id=1, source_target_pairs={{0,4},{4,8},{8,12},{12,16},{16,20},{20,24},{24,28},{1,5},{5,9},{9,... | collective-permute-start | bytes 589832 | tf_op jit(solution)/shard_map/while/body/eval_jaxpr/ppermute | solution.py:26
  528.1 10.1 collective-permute-start.1
  531.5 6.7 collective-permute-start.2
  540.5 26.0 %collective-permute-start.3 = (bf16[512,3,64]{0,2,1:T(8,128)(2,1)S(1)}, bf16[512,3,64]{0,2,1:T(8,128)(2,1)S(1)}, u32[]{:S(2)}, u32[]{:S(2)}) collective-permute-start(bf16[512,3,64]{0,2,1:T(8,128)(2,1)S(1)} %convert_element_type.482), channel_id=1, source_target_pairs={{28,0},{0,4},{4,8},{8,12},{12,16},{16,20},{20,24},{24,28},{29,1},{... | collective-permute-start | bytes 589832 | tf_op jit(solution)/shard_map/while/body/eval_jaxpr/ppermute | solution.py:32
  554.9 11.7 %collective-permute-start.4 = (bf16[512,3,64]{0,2,1:T(8,128)(2,1)S(1)}, bf16[512,3,64]{0,2,1:T(8,128)(2,1)S(1)}, u32[]{:S(2)}, u32[]{:S(2)}) collective-permute-start(bf16[512,3,64]{0,2,1:T(8,128)(2,1)S(1)} %convert_element_type.484), channel_id=1, source_target_pairs={{28,0},{0,4},{4,8},{8,12},{12,16},{16,20},{20,24},{24,28},{29,1},{... | collective-permute-start | bytes 589832 | tf_op jit(solution)/shard_map/while/body/eval_jaxpr/ppermute | solution.py:32
  557.3 12.5 %collective-permute-start = (bf16[512,3,64]{0,2,1:T(8,128)(2,1)}, bf16[512,3,64]{0,2,1:T(8,128)(2,1)S(1)}, u32[]{:S(2)}, u32[]{:S(2)}) collective-permute-start(bf16[512,3,64]{0,2,1:T(8,128)(2,1)} %copy.212), channel_id=1, source_target_pairs={{0,4},{4,8},{8,12},{12,16},{16,20},{20,24},{24,28},{1,5},{5,9},{9,... | collective-permute-start | bytes 589832 | tf_op jit(solution)/shard_map/while/body/eval_jaxpr/ppermute | solution.py:26
  559.8 10.0 collective-permute-start.1
  564.1 5.7 collective-permute-start.2
  572.0 26.0 %collective-permute-start.3 = (bf16[512,3,64]{0,2,1:T(8,128)(2,1)S(1)}, bf16[512,3,64]{0,2,1:T(8,128)(2,1)S(1)}, u32[]{:S(2)}, u32[]{:S(2)}) collective-permute-start(bf16[512,3,64]{0,2,1:T(8,128)(2,1)S(1)} %convert_element_type.482), channel_id=1, source_target_pairs={{28,0},{0,4},{4,8},{8,12},{12,16},{16,20},{20,24},{24,28},{29,1},{... | collective-permute-start | bytes 589832 | tf_op jit(solution)/shard_map/while/body/eval_jaxpr/ppermute | solution.py:32
  575.5 22.6 %collective-permute-start.4 = (bf16[512,3,64]{0,2,1:T(8,128)(2,1)S(1)}, bf16[512,3,64]{0,2,1:T(8,128)(2,1)S(1)}, u32[]{:S(2)}, u32[]{:S(2)}) collective-permute-start(bf16[512,3,64]{0,2,1:T(8,128)(2,1)S(1)} %convert_element_type.484), channel_id=1, source_target_pairs={{28,0},{0,4},{4,8},{8,12},{12,16},{16,20},{20,24},{24,28},{29,1},{... | collective-permute-start | bytes 589832 | tf_op jit(solution)/shard_map/while/body/eval_jaxpr/ppermute | solution.py:32
  589.0 11.0 %collective-permute-start = (bf16[512,3,64]{0,2,1:T(8,128)(2,1)}, bf16[512,3,64]{0,2,1:T(8,128)(2,1)S(1)}, u32[]{:S(2)}, u32[]{:S(2)}) collective-permute-start(bf16[512,3,64]{0,2,1:T(8,128)(2,1)} %copy.212), channel_id=1, source_target_pairs={{0,4},{4,8},{8,12},{12,16},{16,20},{20,24},{24,28},{1,5},{5,9},{9,... | collective-permute-start | bytes 589832 | tf_op jit(solution)/shard_map/while/body/eval_jaxpr/ppermute | solution.py:26
  591.3 8.7 collective-permute-start.1
  602.2 27.0 %collective-permute-start.3 = (bf16[512,3,64]{0,2,1:T(8,128)(2,1)S(1)}, bf16[512,3,64]{0,2,1:T(8,128)(2,1)S(1)}, u32[]{:S(2)}, u32[]{:S(2)}) collective-permute-start(bf16[512,3,64]{0,2,1:T(8,128)(2,1)S(1)} %convert_element_type.482), channel_id=1, source_target_pairs={{28,0},{0,4},{4,8},{8,12},{12,16},{16,20},{20,24},{24,28},{29,1},{... | collective-permute-start | bytes 589832 | tf_op jit(solution)/shard_map/while/body/eval_jaxpr/ppermute | solution.py:32
  605.7 23.6 %collective-permute-start.4 = (bf16[512,3,64]{0,2,1:T(8,128)(2,1)S(1)}, bf16[512,3,64]{0,2,1:T(8,128)(2,1)S(1)}, u32[]{:S(2)}, u32[]{:S(2)}) collective-permute-start(bf16[512,3,64]{0,2,1:T(8,128)(2,1)S(1)} %convert_element_type.484), channel_id=1, source_target_pairs={{28,0},{0,4},{4,8},{8,12},{12,16},{16,20},{20,24},{24,28},{29,1},{... | collective-permute-start | bytes 589832 | tf_op jit(solution)/shard_map/while/body/eval_jaxpr/ppermute | solution.py:32
  609.0 21.5 %collective-permute-start = (bf16[512,3,64]{0,2,1:T(8,128)(2,1)}, bf16[512,3,64]{0,2,1:T(8,128)(2,1)S(1)}, u32[]{:S(2)}, u32[]{:S(2)}) collective-permute-start(bf16[512,3,64]{0,2,1:T(8,128)(2,1)} %copy.212), channel_id=1, source_target_pairs={{0,4},{4,8},{8,12},{12,16},{16,20},{20,24},{24,28},{1,5},{5,9},{9,... | collective-permute-start | bytes 589832 | tf_op jit(solution)/shard_map/while/body/eval_jaxpr/ppermute | solution.py:26
  622.5 8.1 collective-permute-start.1
  632.8 26.8 %collective-permute-start.3 = (bf16[512,3,64]{0,2,1:T(8,128)(2,1)S(1)}, bf16[512,3,64]{0,2,1:T(8,128)(2,1)S(1)}, u32[]{:S(2)}, u32[]{:S(2)}) collective-permute-start(bf16[512,3,64]{0,2,1:T(8,128)(2,1)S(1)} %convert_element_type.482), channel_id=1, source_target_pairs={{28,0},{0,4},{4,8},{8,12},{12,16},{16,20},{20,24},{24,28},{29,1},{... | collective-permute-start | bytes 589832 | tf_op jit(solution)/shard_map/while/body/eval_jaxpr/ppermute | solution.py:32
  636.1 23.5 %collective-permute-start.4 = (bf16[512,3,64]{0,2,1:T(8,128)(2,1)S(1)}, bf16[512,3,64]{0,2,1:T(8,128)(2,1)S(1)}, u32[]{:S(2)}, u32[]{:S(2)}) collective-permute-start(bf16[512,3,64]{0,2,1:T(8,128)(2,1)S(1)} %convert_element_type.484), channel_id=1, source_target_pairs={{28,0},{0,4},{4,8},{8,12},{12,16},{16,20},{20,24},{24,28},{29,1},{... | collective-permute-start | bytes 589832 | tf_op jit(solution)/shard_map/while/body/eval_jaxpr/ppermute | solution.py:32
  639.3 22.4 %collective-permute-start = (bf16[512,3,64]{0,2,1:T(8,128)(2,1)}, bf16[512,3,64]{0,2,1:T(8,128)(2,1)S(1)}, u32[]{:S(2)}, u32[]{:S(2)}) collective-permute-start(bf16[512,3,64]{0,2,1:T(8,128)(2,1)} %copy.212), channel_id=1, source_target_pairs={{0,4},{4,8},{8,12},{12,16},{16,20},{20,24},{24,28},{1,5},{5,9},{9,... | collective-permute-start | bytes 589832 | tf_op jit(solution)/shard_map/while/body/eval_jaxpr/ppermute | solution.py:26
  642.5 19.2 %collective-permute-start.1 = (bf16[512,3,64]{0,2,1:T(8,128)(2,1)}, bf16[512,3,64]{0,2,1:T(8,128)(2,1)S(1)}, u32[]{:S(2)}, u32[]{:S(2)}) collective-permute-start(bf16[512,3,64]{0,2,1:T(8,128)(2,1)} %copy.213), channel_id=1, source_target_pairs={{0,4},{4,8},{8,12},{12,16},{16,20},{20,24},{24,28},{1,5},{5,9},{9,... | collective-permute-start | bytes 589832 | tf_op jit(solution)/shard_map/while/body/eval_jaxpr/ppermute | solution.py:26
  657.5 4.2 collective-permute-start.2
  663.9 25.0 %collective-permute-start.3 = (bf16[512,3,64]{0,2,1:T(8,128)(2,1)S(1)}, bf16[512,3,64]{0,2,1:T(8,128)(2,1)S(1)}, u32[]{:S(2)}, u32[]{:S(2)}) collective-permute-start(bf16[512,3,64]{0,2,1:T(8,128)(2,1)S(1)} %convert_element_type.482), channel_id=1, source_target_pairs={{28,0},{0,4},{4,8},{8,12},{12,16},{16,20},{20,24},{24,28},{29,1},{... | collective-permute-start | bytes 589832 | tf_op jit(solution)/shard_map/while/body/eval_jaxpr/ppermute | solution.py:32
  667.4 21.6 %collective-permute-start.4 = (bf16[512,3,64]{0,2,1:T(8,128)(2,1)S(1)}, bf16[512,3,64]{0,2,1:T(8,128)(2,1)S(1)}, u32[]{:S(2)}, u32[]{:S(2)}) collective-permute-start(bf16[512,3,64]{0,2,1:T(8,128)(2,1)S(1)} %convert_element_type.484), channel_id=1, source_target_pairs={{28,0},{0,4},{4,8},{8,12},{12,16},{16,20},{20,24},{24,28},{29,1},{... | collective-permute-start | bytes 589832 | tf_op jit(solution)/shard_map/while/body/eval_jaxpr/ppermute | solution.py:32
  669.2 21.1 %collective-permute-start = (bf16[512,3,64]{0,2,1:T(8,128)(2,1)}, bf16[512,3,64]{0,2,1:T(8,128)(2,1)S(1)}, u32[]{:S(2)}, u32[]{:S(2)}) collective-permute-start(bf16[512,3,64]{0,2,1:T(8,128)(2,1)} %copy.212), channel_id=1, source_target_pairs={{0,4},{4,8},{8,12},{12,16},{16,20},{20,24},{24,28},{1,5},{5,9},{9,... | collective-permute-start | bytes 589832 | tf_op jit(solution)/shard_map/while/body/eval_jaxpr/ppermute | solution.py:26
  671.2 19.0 %collective-permute-start.1 = (bf16[512,3,64]{0,2,1:T(8,128)(2,1)}, bf16[512,3,64]{0,2,1:T(8,128)(2,1)S(1)}, u32[]{:S(2)}, u32[]{:S(2)}) collective-permute-start(bf16[512,3,64]{0,2,1:T(8,128)(2,1)} %copy.213), channel_id=1, source_target_pairs={{0,4},{4,8},{8,12},{12,16},{16,20},{20,24},{24,28},{1,5},{5,9},{9,... | collective-permute-start | bytes 589832 | tf_op jit(solution)/shard_map/while/body/eval_jaxpr/ppermute | solution.py:26
  676.4 13.8 %collective-permute-start.2 = (s32[512]{0:T(512)S(1)}, s32[512]{0:T(512)S(1)}, u32[]{:S(2)}, u32[]{:S(2)}) collective-permute-start(s32[512]{0:T(512)S(1)} %copy.214), channel_id=1, source_target_pairs={{0,4},{4,8},{8,12},{12,16},{16,20},{20,24},{24,28},{1,5},{5,9},{9,... | collective-permute-start | bytes 6152 | tf_op jit(solution)/shard_map/while/body/eval_jaxpr/ppermute | solution.py:26
  692.5 16.0 %collective-permute-start.3 = (bf16[512,3,64]{0,2,1:T(8,128)(2,1)S(1)}, bf16[512,3,64]{0,2,1:T(8,128)(2,1)S(1)}, u32[]{:S(2)}, u32[]{:S(2)}) collective-permute-start(bf16[512,3,64]{0,2,1:T(8,128)(2,1)S(1)} %convert_element_type.482), channel_id=1, source_target_pairs={{28,0},{0,4},{4,8},{8,12},{12,16},{16,20},{20,24},{24,28},{29,1},{... | collective-permute-start | bytes 589832 | tf_op jit(solution)/shard_map/while/body/eval_jaxpr/ppermute | solution.py:32
  695.9 14.7 %collective-permute-start.4 = (bf16[512,3,64]{0,2,1:T(8,128)(2,1)S(1)}, bf16[512,3,64]{0,2,1:T(8,128)(2,1)S(1)}, u32[]{:S(2)}, u32[]{:S(2)}) collective-permute-start(bf16[512,3,64]{0,2,1:T(8,128)(2,1)S(1)} %convert_element_type.484), channel_id=1, source_target_pairs={{28,0},{0,4},{4,8},{8,12},{12,16},{16,20},{20,24},{24,28},{29,1},{... | collective-permute-start | bytes 589832 | tf_op jit(solution)/shard_map/while/body/eval_jaxpr/ppermute | solution.py:32
  698.2 12.5 %collective-permute-start = (bf16[512,3,64]{0,2,1:T(8,128)(2,1)}, bf16[512,3,64]{0,2,1:T(8,128)(2,1)S(1)}, u32[]{:S(2)}, u32[]{:S(2)}) collective-permute-start(bf16[512,3,64]{0,2,1:T(8,128)(2,1)} %copy.212), channel_id=1, source_target_pairs={{0,4},{4,8},{8,12},{12,16},{16,20},{20,24},{24,28},{1,5},{5,9},{9,... | collective-permute-start | bytes 589832 | tf_op jit(solution)/shard_map/while/body/eval_jaxpr/ppermute | solution.py:26
  701.0 9.7 collective-permute-start.1
  703.0 7.7 collective-permute-start.2
  713.0 23.3 %collective-permute-start.3 = (bf16[512,3,64]{0,2,1:T(8,128)(2,1)S(1)}, bf16[512,3,64]{0,2,1:T(8,128)(2,1)S(1)}, u32[]{:S(2)}, u32[]{:S(2)}) collective-permute-start(bf16[512,3,64]{0,2,1:T(8,128)(2,1)S(1)} %convert_element_type.482), channel_id=1, source_target_pairs={{28,0},{0,4},{4,8},{8,12},{12,16},{16,20},{20,24},{24,28},{29,1},{... | collective-permute-start | bytes 589832 | tf_op jit(solution)/shard_map/while/body/eval_jaxpr/ppermute | solution.py:32
  723.3 15.1 %collective-permute-start.4 = (bf16[512,3,64]{0,2,1:T(8,128)(2,1)S(1)}, bf16[512,3,64]{0,2,1:T(8,128)(2,1)S(1)}, u32[]{:S(2)}, u32[]{:S(2)}) collective-permute-start(bf16[512,3,64]{0,2,1:T(8,128)(2,1)S(1)} %convert_element_type.484), channel_id=1, source_target_pairs={{28,0},{0,4},{4,8},{8,12},{12,16},{16,20},{20,24},{24,28},{29,1},{... | collective-permute-start | bytes 589832 | tf_op jit(solution)/shard_map/while/body/eval_jaxpr/ppermute | solution.py:32
  726.6 11.8 %collective-permute-start = (bf16[512,3,64]{0,2,1:T(8,128)(2,1)}, bf16[512,3,64]{0,2,1:T(8,128)(2,1)S(1)}, u32[]{:S(2)}, u32[]{:S(2)}) collective-permute-start(bf16[512,3,64]{0,2,1:T(8,128)(2,1)} %copy.212), channel_id=1, source_target_pairs={{0,4},{4,8},{8,12},{12,16},{16,20},{20,24},{24,28},{1,5},{5,9},{9,... | collective-permute-start | bytes 589832 | tf_op jit(solution)/shard_map/while/body/eval_jaxpr/ppermute | solution.py:26
  730.0 8.5 collective-permute-start.1
  732.9 5.5 collective-permute-start.2
  743.2 116.9 %reduce-scatter.15.cloned.1.call-start = ((), (), s32[]{:S(2)}) async-start(), calls=%async_computation.12 | async-start | bytes 884736
  748.1 181.2 %reduce-scatter.13.cloned.1.call-start = ((), (), s32[]{:S(2)}) async-start(), calls=%async_computation.11 | async-start | bytes 2211840
  764.6 237.1 %reduce-scatter.9.cloned.1.call-start = ((), (), s32[]{:S(2)}) async-start(), calls=%async_computation.9 | async-start | bytes 2654208 | tf_op jit(solution)/shard_map/reduce_scatter | solution.py:397
  768.4 305.6 %reduce-scatter.11.cloned.1.call-start = ((), (), s32[]{:S(2)}) async-start(), calls=%async_computation.10 | async-start | bytes 2654208 | tf_op jit(solution)/shard_map/reduce_scatter | solution.py:398
  (112 other events, 1248.5 us)
Sparse Core Ops, SparseCore 0:
  15.0 48.1 all-gather.5
  65.9 43.6 all-gather.3
  113.4 209.7 all-reduce.7
  417.8 33.5 all-reduce.9
  461.3 34.6 all-reduce.11
  743.3 50.5 all-reduce.13
  797.5 62.5 reduce-scatter.14
  863.6 65.6 reduce-scatter.12
  933.8 67.8 reduce-scatter.8
  1006.0 68.0 reduce-scatter.10
where the time goes:
time: 1090 us; the launch traced here: 1080 us
  waiting for transfers between devices  376 us (34%)
  other arithmetic  178 us (16%)
  starting transfers between devices  174 us (16%)
  matrix products  134 us (12%)
  local copies, waits for them, and re-layouts  115 us (11%)
  blocking collectives  66.9 us (6%)
  between operations  20.4 us (2%)
  loops' own time  17 us (2%)
    ppermute x24, starting transfers between devices, shifted(): return lax.ppermute(block, axis, route)  105 us
    unnamed x12, waiting for transfers between devices  88.5 us
    another operation x15, other arithmetic, local(): jnp.linalg.cholesky(book_gram_matrix + RIDGE * jnp.eye(NB, dtype=jnp.floa...  85.1 us
    reduce_scatter x1, waiting for transfers between devices, local(): lax.psum_scatter(grad_proj_w, 'seq', scatter_dimension=1, tiled=True)  72.4 us
    reduce_scatter x1, waiting for transfers between devices, local(): lax.psum_scatter(grad_fc_w, 'seq', scatter_dimension=0, tiled=True)  70.4 us
    ppermute x16, starting transfers between devices, passed_along(): return lax.ppermute(block, axis, route)  67.6 us
    psum x1, waiting for transfers between devices, local(): lax.psum(jnp.einsum('sb,snd->bnd', past_member, proj_seg, precision=UPPER...  51.2 us
    another operation x4, other arithmetic, solve_one(): return jax.scipy.linalg.cho_solve((factor, True), rhs_mat)  44.8 us
  transfers between devices with their start and end apart: 50, of which 18 were waited for; matrix products, arithmetic and copies ran while one was open for 24% of the time, Pallas kernels for 0%

commit v1 on v0

--- a/solution.py
+++ b/solution.py
@@ -1,4 +1,7 @@
 import math
+
+import ml_dtypes
+import numpy as np
 
 import jax
 import jax.numpy as jnp
@@ -55,34 +58,18 @@
     return jnp.exp(-0.5 * offset * offset)
 
 
-def memory_density(affinity, mu_weight, sigma_weight):
-    basis_n = mu_weight.shape[1]
-    rbf_width = 1.0 / basis_n
-    centre = jax.nn.sigmoid(
-        jnp.einsum("...hn,hn->...h", affinity, mu_weight, precision=UPPER_LIMIT)
-    )
-    unconstrained_spread = jnp.einsum(
-        "...hn,hn->...h", affinity, sigma_weight, precision=UPPER_LIMIT
-    )
-    spread_sq = SPREAD * jax.nn.softplus(unconstrained_spread) + rbf_width * rbf_width
-    centre_gap = centre[..., None] - radial_centres(basis_n)
-    return (
-        rbf_width
-        * lax.rsqrt(spread_sq)[..., None]
-        * jnp.exp(-0.5 * centre_gap * centre_gap / spread_sq[..., None])
-    )
-
-
-def shared_solver(factor):
-
-    def solve_all(rhs_books):
-
-        def solve_one(rhs_mat):
-            return jax.scipy.linalg.cho_solve((factor, True), rhs_mat)
-
-        return jax.vmap(solve_one)(rhs_books)
-
-    return solve_all
+def coefficient_tables(age_count, basis_n, seg_len):
+    shrink = TAU ** np.arange(age_count, dtype=np.float64)
+    inside = (np.arange(seg_len) + 0.5) / seg_len
+    times = shrink[:, None] * (TAU + (1.0 - TAU) * inside[None, :])
+    centres = (np.arange(basis_n) + 0.5) / basis_n
+    offset = (times[:, None, :] - centres[None, :, None]) * basis_n
+    basis = np.exp(-0.5 * offset * offset)
+    gram = np.einsum("agx,ahx->gh", basis, basis) + RIDGE * np.eye(basis_n)
+    table = np.linalg.solve(gram[None], basis)
+    high = table.astype(ml_dtypes.bfloat16)
+    lower = (table - high.astype(np.float64)).astype(ml_dtypes.bfloat16)
+    return high, lower
 
 
 def block_rows(row_count_total, tok_rows):
@@ -173,30 +160,39 @@
     scale_dh = DH ** (-0.5)
     head_shape = (tok_rows, heads_here, DH)
     own_pos = seq_index * tok_rows + jnp.arange(tok_rows, dtype=jnp.int32)
-    book_ids = jnp.arange(BOOKS, dtype=jnp.int32)
-    past_member = (past_book[:, None] == book_ids[None, :]).astype(jnp.float32)
-    read_member = (cur_book[:, None] == book_ids[None, :]).astype(jnp.bfloat16)
-    all_ages = jnp.arange(seq_count * seg_here // BOOKS, dtype=jnp.int32)
-    basis_of_ages = past_basis(all_ages, NB, SEG)
-    book_gram_matrix = jnp.einsum(
-        "fgx,fhx->gh", basis_of_ages, basis_of_ages, precision=UPPER_LIMIT
-    )
-    factor = jnp.linalg.cholesky(book_gram_matrix + RIDGE * jnp.eye(NB, dtype=jnp.float32))
-    solve_all = shared_solver(factor)
-    past_rows = past_states.reshape(seg_here, SEG, D).astype(jnp.float32)
-    basis_vals = past_basis(past_age, NB, SEG)
-    proj_seg = jnp.einsum("snt,std->snd", basis_vals, past_rows, precision=UPPER_LIMIT)
-    kv_weight = qkv_weight[:, 1:].astype(jnp.float32).reshape(D, 2 * head_cols)
-    proj_sum = lax.psum(
-        jnp.einsum("sb,snd->bnd", past_member, proj_seg, precision=UPPER_LIMIT), "seq"
-    )
-    coeffs = solve_all(proj_sum)
-    mem_kv = jnp.einsum("bnd,dm->bnm", coeffs, kv_weight, precision=UPPER_LIMIT)
-    mem_seg = jnp.einsum(
-        "sb,bnm->snm", read_member, mem_kv.astype(jnp.bfloat16), preferred_element_type=jnp.float32
+    quarter = D // lax.axis_size("tp")
+    my_quarter = lax.dynamic_slice_in_dim(
+        past_states, lax.axis_index("tp") * quarter, quarter, axis=1
+    )
+    all_states = lax.all_gather(my_quarter, "seq", axis=0)
+    books_ages = lax.all_gather(jnp.stack([past_book, past_age]), "seq", axis=1, tiled=True)
+    age_count = seq_count * seg_here // BOOKS
+    high, lower = coefficient_tables(age_count, NB, SEG)
+    chosen = (books_ages[0] == cur_book[0])[None, :] & (
+        books_ages[1][None, :] == jnp.arange(age_count, dtype=jnp.int32)[:, None]
+    )
+    by_age = jnp.einsum(
+        "as,std->atd",
+        chosen.astype(jnp.bfloat16),
+        all_states,
+        preferred_element_type=jnp.float32,
     ).astype(jnp.bfloat16)
-    mem_keys = mem_seg[:, :, :head_cols].reshape(seg_here, NB, heads_here, DH)
-    mem_vals = mem_seg[:, :, head_cols:].reshape(seg_here, NB, heads_here, DH)
+    coeff_part = jnp.einsum(
+        "ant,atd->nd", jnp.asarray(high), by_age, preferred_element_type=jnp.float32
+    ) + jnp.einsum("ant,atd->nd", jnp.asarray(lower), by_age, preferred_element_type=jnp.float32)
+    coeffs = lax.all_gather(coeff_part.astype(jnp.bfloat16), "tp", axis=1, tiled=True)
+    mem_keys = (
+        jnp.dot(coeffs, qkv_weight[:, 1], preferred_element_type=jnp.float32)
+        .astype(jnp.bfloat16)
+        .reshape(NB, heads_here, DH)
+    )
+    mem_vals = (
+        jnp.dot(coeffs, qkv_weight[:, 2], preferred_element_type=jnp.float32)
+        .astype(jnp.bfloat16)
+        .reshape(NB, heads_here, DH)
+    )
+    key_mu = jnp.einsum("nhd,hn->hd", mem_keys.astype(jnp.float32), mu_weight, precision=UPPER_LIMIT) * scale_dh
+    key_sigma = jnp.einsum("nhd,hn->hd", mem_keys.astype(jnp.float32), sigma_weight, precision=UPPER_LIMIT) * scale_dh
     hidden_in = tokens.astype(jnp.float32)
     normed_one_f, norm_one_back = jax.vjp(layer_norm, hidden_in, ln1_gain, ln1_bias)
     normed_one = normed_one_f.astype(jnp.bfloat16)
@@ -226,16 +222,20 @@
     )
     log_sum = row_max + jnp.log(row_sum)
     local_out = accumulated / row_sum[..., None]
-    seg_queries = queries.reshape(seg_here, SEG, heads_here, DH)
-    affinity = (
-        jnp.einsum("sthd,snhd->sthn", seg_queries, mem_keys, preferred_element_type=jnp.float32)
-        * scale_dh
-    )
-    density, density_back = jax.vjp(memory_density, affinity, mu_weight, sigma_weight)
-    density_bf = density.astype(jnp.bfloat16)
+    rbf_width = 1.0 / NB
+    queries_f = queries.astype(jnp.float32)
+    centre = jax.nn.sigmoid(jnp.sum(queries_f * key_mu, axis=-1))
+    loose = jnp.sum(queries_f * key_sigma, axis=-1)
+    spread_sq = SPREAD * jax.nn.softplus(loose) + rbf_width * rbf_width
+    gap = centre[..., None] - radial_centres(NB)
+    density_bf = (
+        rbf_width
+        * lax.rsqrt(spread_sq)[..., None]
+        * jnp.exp(-0.5 * gap * gap / spread_sq[..., None])
+    ).astype(jnp.bfloat16)
     mem_out = jnp.einsum(
-        "sthn,snhd->sthd", density_bf, mem_vals, preferred_element_type=jnp.float32
-    ).reshape(head_shape)
+        "thn,nhd->thd", density_bf, mem_vals, preferred_element_type=jnp.float32
+    )
     heads_out = (local_out + mem_out).astype(jnp.bfloat16).reshape(tok_rows, head_cols)
     branch_one = (
         lax.psum(
@@ -283,35 +283,32 @@
         .astype(jnp.bfloat16)
         .reshape(head_shape)
     )
-    seg_grad = grad_heads.reshape(seg_here, SEG, heads_here, DH)
     grad_density = jnp.einsum(
-        "sthd,snhd->sthn", seg_grad, mem_vals, preferred_element_type=jnp.float32
+        "thd,nhd->thn", grad_heads, mem_vals, preferred_element_type=jnp.float32
     )
     grad_mem_vals = jnp.einsum(
-        "sthn,sthd->snhd", density_bf, seg_grad, preferred_element_type=jnp.float32
-    )
-    grad_aff, grad_mu_w, grad_sigma_w = density_back(grad_density)
-    aff_bf = grad_aff.astype(jnp.bfloat16)
-    grad_q_mem = (
-        jnp.einsum("sthn,snhd->sthd", aff_bf, mem_keys, preferred_element_type=jnp.float32).reshape(
-            head_shape
-        )
-        * scale_dh
-    )
+        "thn,thd->nhd", density_bf, grad_heads, preferred_element_type=jnp.float32
+    )
+    weighed = grad_density * density_bf.astype(jnp.float32)
+    sum_gap = jnp.sum(weighed * gap, axis=-1)
+    sum_gap_sq = jnp.sum(weighed * gap * gap, axis=-1)
+    sum_zero = jnp.sum(weighed, axis=-1)
+    grad_centre = -sum_gap / spread_sq
+    grad_spread = 0.5 * (sum_gap_sq / spread_sq - sum_zero) / spread_sq
+    pull_mu = grad_centre * centre * (1.0 - centre)
+    pull_sigma = grad_spread * SPREAD * jax.nn.sigmoid(loose)
+    grad_q_mem = pull_mu[..., None] * key_mu + pull_sigma[..., None] * key_sigma
+    query_mu = jnp.sum(pull_mu[..., None] * queries_f, axis=0) * scale_dh
+    query_sigma = jnp.sum(pull_sigma[..., None] * queries_f, axis=0) * scale_dh
+    mem_keys_f = mem_keys.astype(jnp.float32)
+    grad_mu_w = jnp.einsum("nhd,hd->hn", mem_keys_f, query_mu, precision=UPPER_LIMIT)
+    grad_sigma_w = jnp.einsum("nhd,hd->hn", mem_keys_f, query_sigma, precision=UPPER_LIMIT)
     grad_mem_keys = (
-        jnp.einsum("sthn,sthd->snhd", aff_bf, seg_queries, preferred_element_type=jnp.float32)
-        * scale_dh
+        mu_weight.T[:, :, None] * query_mu[None] + sigma_weight.T[:, :, None] * query_sigma[None]
     )
     grad_mem_seg = jnp.concatenate(
-        [
-            grad_mem_keys.reshape(seg_here, NB, head_cols),
-            grad_mem_vals.reshape(seg_here, NB, head_cols),
-        ],
-        axis=-1,
-    )
-    grad_mem_books = jnp.einsum(
-        "sb,snm->bnm", read_member.astype(jnp.float32), grad_mem_seg, precision=UPPER_LIMIT
-    )
+        [grad_mem_keys.reshape(NB, head_cols), grad_mem_vals.reshape(NB, head_cols)], axis=-1
+    ).astype(jnp.bfloat16)
     row_delta = jnp.sum(grad_heads.astype(jnp.float32) * local_out, axis=-1)
 
     def cycle_step(step, carry):
@@ -375,7 +372,7 @@
     grad_v_bf = grad_vals.astype(jnp.bfloat16).reshape(tok_rows, head_cols)
     grad_qkv = jnp.stack([grad_q_bf, grad_k_bf, grad_v_bf], axis=1)
     grad_qkv_w = jnp.einsum("td,tcm->dcm", normed_one, grad_qkv, preferred_element_type=jnp.float32)
-    grad_kv_w = jnp.einsum("bnd,bnm->dm", coeffs, grad_mem_books, precision=UPPER_LIMIT)
+    grad_kv_w = jnp.einsum("nd,nm->dm", coeffs, grad_mem_seg, preferred_element_type=jnp.float32)
     grad_qkv_w = grad_qkv_w.at[:, 1:].add(grad_kv_w.reshape(D, 2, head_cols))
     grad_qv_b = jnp.stack(
         [
@@ -392,10 +389,16 @@
     grad_in_part, grad_ln1_g, grad_ln1_b = norm_one_back(grad_normed_one)
     grad_tokens = (grad_resid + grad_in_part).astype(jnp.bfloat16)
     qkv_share, out_share, fc_share, proj_share = (
-        lax.psum_scatter(grad_qkv_w, "seq", scatter_dimension=0, tiled=True),
-        lax.psum_scatter(grad_out_w, "seq", scatter_dimension=1, tiled=True),
-        lax.psum_scatter(grad_fc_w, "seq", scatter_dimension=0, tiled=True),
-        lax.psum_scatter(grad_proj_w, "seq", scatter_dimension=1, tiled=True),
+        lax.psum_scatter(grad_qkv_w.reshape(D, -1).astype(jnp.bfloat16), "seq", scatter_dimension=0, tiled=True),
+        lax.psum_scatter(grad_out_w.astype(jnp.bfloat16), "seq", scatter_dimension=1, tiled=True),
+        lax.psum_scatter(grad_fc_w.astype(jnp.bfloat16), "seq", scatter_dimension=0, tiled=True),
+        lax.psum_scatter(grad_proj_w.astype(jnp.bfloat16), "seq", scatter_dimension=1, tiled=True),
+    )
+    qkv_share = qkv_share.astype(jnp.float32).reshape(-1, 3, head_cols)
+    out_share, fc_share, proj_share = (
+        out_share.astype(jnp.float32),
+        fc_share.astype(jnp.float32),
+        proj_share.astype(jnp.float32),
     )
     small_sums = lax.psum(
         (

time: 1090 us -> 801 us (0.73)
  other arithmetic: 178 us -> 64.9 us
  matrix products: 134 us -> 42 us
  local copies, waits for them, and re-layouts: 115 us -> 65.5 us
  blocking collectives: 66.9 us -> 96.1 us
  starting transfers between devices: 174 us -> 146 us
  waiting for transfers between devices: 376 us -> 349 us
    another operation x23 -> x1, other arithmetic: 131 us -> 0.81 us  [the longest x15 85.1 us: local(): jnp.linalg.cholesky(book_gram_matrix + RIDGE * jnp.eye(NB, dtype=jnp.floa...]
    unnamed x12, waiting for transfers between devices: 88.5 us -> 19.4 us
    psum x1 -> x0, waiting for transfers between devices: 51.2 us -> none  [local(): lax.psum(jnp.einsum('sb,snd->bnd', past_member, proj_seg, precision=UPPER...]
    another operation x20 -> x0, matrix products: 45.6 us -> none  [the longest x14 38.4 us: solve_one(): return jax.scipy.linalg.cho_solve((factor, True), rhs_mat)]
    psum x1, waiting for transfers between devices: 27.6 us -> 71.7 us  [local(): lax.psum(jnp.dot(heads_out, out_weight, preferred_element_type=jnp.float3...]
    all_gather x1, waiting for transfers between devices: 0.01 us -> 38.8 us  [local(): lax.all_gather(key_rows, 'seq', axis=0, tiled=True)]
    dot_general x15 -> x14, matrix products: 47.8 us -> 10.1 us  [the longest x1 2.34 us: local(): jnp.einsum('thd,nhd->thn', grad_heads, mem_vals, preferred_element_type=j...]
    another operation x22 -> x0, local copies, waits for them, and re-layouts: 34.2 us -> none  [the longest x6 19.5 us: solve_one(): return jax.scipy.linalg.cho_solve((factor, True), rhs_mat)]
  transfers between devices with their start and end apart: 50 -> 50, of which waited for: 18 -> 13; matrix products, arithmetic and copies ran while one was open for 24% -> 15% of each run, Pallas kernels for 0% -> 0%
where the time goes in v1:
time: 801 us; the launch traced here: 798 us
  waiting for transfers between devices  349 us (44%)
  starting transfers between devices  146 us (18%)
  blocking collectives  96.1 us (12%)
  local copies, waits for them, and re-layouts  65.5 us (8%)
  other arithmetic  64.9 us (8%)
  matrix products  42 us (5%)
  between operations  17.2 us (2%)
  loops' own time  17 us (2%)
    ppermute x24, starting transfers between devices, shifted(): return lax.ppermute(block, axis, route)  82.2 us
    psum x1, waiting for transfers between devices, local(): lax.psum(jnp.dot(heads_out, out_weight, preferred_element_type=jnp.float3...  71.7 us
    reduce_scatter x1, waiting for transfers between devices, local(): lax.psum_scatter(grad_proj_w.astype(jnp.bfloat16), 'seq', scatter_dimensi...  65.2 us
    reduce_scatter x1, waiting for transfers between devices, local(): lax.psum_scatter(grad_fc_w.astype(jnp.bfloat16), 'seq', scatter_dimension...  65.1 us
    ppermute x16, starting transfers between devices, passed_along(): return lax.ppermute(block, axis, route)  62.3 us
    psum x1, blocking collectives, local(): lax.psum((grad_ln1_g, grad_ln1_b, grad_qv_b, grad_out_b, grad_ln2_g, grad...  39.1 us
    all_gather x1, waiting for transfers between devices, local(): lax.all_gather(key_rows, 'seq', axis=0, tiled=True)  38.8 us
    psum x1, waiting for transfers between devices, local(): lax.psum(jnp.einsum('tf,df->td', pre_bf, fc_weight, preferred_element_typ...  30.4 us
  transfers between devices with their start and end apart: 50, of which 13 were waited for; matrix products, arithmetic and copies ran while one was open for 15% of the time, Pallas kernels for 0%

profile of v1, /device:TPU:0, one launch (start us, length us, event | category | flops | bytes accessed | tf_op | source)
XLA Modules:
  0.0 797.6 jit_solution(16316324806882329637)
XLA Ops:
  17.9 22.2 %all-gather.2 = s32[8,1,2]{2,1,0:T(1,128)S(1)} all-gather(s32[1,1,2]{2,1,0:T(1,128)S(1)} %add_bitcast_fusion), channel_id=1, replica_groups=mesh['seq'=8,'tp'=4] {'seq'}, dimensions={0}, use_global_device_ids=true | all-gather | bytes 72 | tf_op jit(solution)/shard_map/all_gather | solution.py:168
  40.1 26.3 %all-gather.1 = s32[8,1,512]{2,1,0:T(1,128)S(1)} all-gather(s32[1,1,512]{2,1,0:T(1,128)S(1)} %bitcast.261), channel_id=1, replica_groups=mesh['seq'=8,'tp'=4] {'seq'}, dimensions={0}, use_global_device_ids=true | all-gather | bytes 18432 | tf_op jit(solution)/shard_map/all_gather | solution.py:220
  67.6 3.1 copy.91
  70.7 38.8 %all-gather.7.cloned.1.call-done = bf16[4096,3,64]{0,2,1:T(8,128)(2,1)} async-done(((bf16[512,3,64]{0,2,1:T(8,128)(2,1)}), bf16[4096,3,64]{0,2,1:T(8,128)(2,1)}) %all-gather.7.cloned.1.call-update) | async-done | bytes 1572880 | tf_op jit(solution)/shard_map/all_gather | solution.py:218
  114.5 8.6 %all_gather.27 = bf16[512,768]{0,1:T(8,128)(2,1)S(1)} all-gather(bf16[512,192]{0,1:T(8,128)(2,1)S(1)} %fusion.95), channel_id=1, replica_groups=mesh['seq'=8,'tp'=4] {'tp'}, dimensions={1}, use_global_device_ids=true | all-gather | bytes 983040 | tf_op jit(solution)/shard_map/all_gather | solution.py:183
  124.7 30.3 %all-gather.9.cloned.1.call-done = bf16[4096,3,64]{0,2,1:T(8,128)(2,1)} async-done(((bf16[512,3,64]{0,2,1:T(8,128)(2,1)}), bf16[4096,3,64]{0,2,1:T(8,128)(2,1)}) %all-gather.9.cloned.1.call-update) | async-done | bytes 1572880 | tf_op jit(solution)/shard_map/all_gather | solution.py:219
  155.0 2.8 copy.114
  158.2 41.1 %while.41 = (s32[]{:T(128)}, f32[512,3]{0,1:T(4,128)S(1)}, f32[512,3]{0,1:T(4,128)S(1)}, f32[512,3,64]{0,2,1:T(8,128)S(1)}, s32[8]{0:T(128)S(1)}, /*index=5*/s32...) while((s32[]{:T(128)}, f32[512,3]{0,1:T(4,128)S(1)}, ...), condition=%wide.region_7.8_spmd, body=%wide.region_2.7_spmd.sunk | while | flops 212536832 | bytes 11976019 | solution.py:127
  162.5 6.2 conditional.5
  203.8 3.3 fusion.142
  207.1 71.7 %all-reduce.6.cloned.1.call-done = bf16[512,768]{1,0:T(8,128)(2,1)} async-done(((bf16[512,768]{1,0:T(8,128)(2,1)}), bf16[512,768]{1,0:T(8,128)(2,1)}) %all-reduce.6.cloned.1.call-update) | async-done | bytes 786448 | tf_op jit(solution)/shard_map/psum | solution.py:241
  281.5 3.6 convert_reduce_fusion.4
  288.5 3.7 convolution_convert_fusion.3
  292.2 30.4 %all-reduce.8.cloned.1.call-done = bf16[512,768]{1,0:T(8,128)(2,1)} async-done(((bf16[512,768]{1,0:T(8,128)(2,1)}), bf16[512,768]{1,0:T(8,128)(2,1)}) %all-reduce.8.cloned.1.call-update) | async-done | bytes 786448 | tf_op jit(solution)/shard_map/psum | solution.py:270
  333.5 197.7 %while.42 = (s32[]{:T(128)}, bf16[512,3,64]{0,2,1:T(8,128)(2,1)S(1)}, bf16[512,3,64]{0,2,1:T(8,128)(2,1)}, s32[512]{0:T(512)S(1)}, f32[512,3,64]{0,2,1:T(8,128)}...) while((s32[]{:T(128)}, ...), condition=%wide.region_21.22_spmd.clone, body=%wide.region_18.21_spmd.clone.sunk | while | flops 514622464 | bytes 28214064 | solution.py:368
  335.3 4.8 conditional.6
  343.9 3.4 collective-permute-start
  347.2 4.1 collective-permute-start.1
  356.2 2.9 collective-permute-done.2
  362.7 8.2 %collective-permute-start.4 = (bf16[512,3,64]{0,2,1:T(8,128)(2,1)}, bf16[512,3,64]{0,2,1:T(8,128)(2,1)S(1)}, u32[]{:S(2)}, u32[]{:S(2)}) collective-permute-start(bf16[512,3,64]{0,2,1:T(8,128)(2,1)} %convert_element_type.527), channel_id=1, source_target_pairs={{28,0},{0,4},{4,8},{8,12},{12,16},{16,20},{20,24},{24,28},{29,1},{... | collective-permute-start | bytes 589832 | tf_op jit(solution)/shard_map/while/body/eval_jaxpr/ppermute | solution.py:35
  370.9 3.5 collective-permute-start.3
  376.3 5.6 collective-permute-start.1
  393.2 8.2 %collective-permute-start.3 = (bf16[512,3,64]{0,2,1:T(8,128)(2,1)S(1)}, bf16[512,3,64]{0,2,1:T(8,128)(2,1)S(1)}, u32[]{:S(2)}, u32[]{:S(2)}) collective-permute-start(bf16[512,3,64]{0,2,1:T(8,128)(2,1)S(1)} %convert_element_type.525), channel_id=1, source_target_pairs={{28,0},{0,4},{4,8},{8,12},{12,16},{16,20},{20,24},{24,28},{29,1},{... | collective-permute-start | bytes 589832 | tf_op jit(solution)/shard_map/while/body/eval_jaxpr/ppermute | solution.py:35
  403.4 5.5 collective-permute-start.1
  415.4 5.3 collective-permute-start.4
  420.8 3.4 collective-permute-start.3
  424.2 6.1 collective-permute-start
  430.3 6.0 collective-permute-start.1
  442.8 3.0 collective-permute-start.4
  445.8 2.9 collective-permute-start.3
  451.2 10.7 %collective-permute-start.1 = (bf16[512,3,64]{0,2,1:T(8,128)(2,1)}, bf16[512,3,64]{0,2,1:T(8,128)(2,1)}, u32[]{:S(2)}, u32[]{:S(2)}) collective-permute-start(bf16[512,3,64]{0,2,1:T(8,128)(2,1)} %copy.154), channel_id=1, source_target_pairs={{0,4},{4,8},{8,12},{12,16},{16,20},{20,24},{24,28},{1,5},{5,9},{9,... | collective-permute-start | bytes 589832 | tf_op jit(solution)/shard_map/while/body/eval_jaxpr/ppermute | solution.py:29
  468.5 2.9 collective-permute-start.4
  471.4 2.9 collective-permute-start.3
  476.2 5.7 collective-permute-start.1
  481.9 5.5 collective-permute-start.2
  492.6 3.4 collective-permute-start.4
  496.1 2.9 collective-permute-start.3
  500.9 3.0 collective-permute-start.1
  512.3 7.4 collective-permute-start.4
  519.7 2.9 collective-permute-start.3
  547.4 3.2 convolution_convert_fusion.1
  551.0 3.4 convolution_convert_fusion
  567.5 20.8 %all-reduce.10.cloned.1.call-done = (bf16[512,768]{1,0:T(8,128)(2,1)}, bf16[512,768]{1,0:T(8,128)(2,1)}) async-done(((bf16[512,768]{1,0:T(8,128)(2,1)}, bf16[512,768]{1,0:T(8,128)(2,1)}), (bf16[512,768]{1,0:T(8,128)(2,1)}, bf16[512,768]{1,0:T(8,128)(2,1)})) %all-reduce.10.cloned.1.call-update) | async-done | bytes 1572880 | tf_op jit(solution)/shard_map/psum | solution.py:254
  593.7 3.2 add_convert_fusion
  596.9 39.1 %all-reduce = (f32[2,192]{1,0:T(2,128)}, f32[768]{0:T(1024)}, f32[768]{0:T(1024)}, f32[768]{0:T(1024)}, f32[768]{0:T(1024)}, /*index=5*/f32[768]{0:T(1024)}, f32...) all-reduce(f32[2,192]{1,0:T(2,128)} %pad_maximum_fusion.1, ...), channel_id=1, replica_groups=mesh['seq'=8,'tp'=4] {'seq'}, use_global_device_ids=true, to_apply=%region_33.34 | all-reduce | flops 8832 | bytes 70656 | tf_op jit(solution)/shard_map/psum | solution.py:403
  636.1 19.2 %reduce-scatter.13.cloned.1.call-done = bf16[96,576]{1,0:T(8,128)(2,1)} async-done(((bf16[768,576]{1,0:T(8,128)(2,1)}), bf16[96,576]{1,0:T(8,128)(2,1)}) %reduce-scatter.13.cloned.1.call-update) | async-done | bytes 110608
  657.2 65.1 %reduce-scatter.9.cloned.1.call-done = bf16[96,768]{1,0:T(8,128)(2,1)} async-done(((bf16[768,768]{1,0:T(8,128)(2,1)}), bf16[96,768]{1,0:T(8,128)(2,1)}) %reduce-scatter.9.cloned.1.call-update) | async-done | bytes 147472 | tf_op jit(solution)/shard_map/reduce_scatter | solution.py:394
  723.9 65.2 %reduce-scatter.11.cloned.1.call-done = bf16[768,96]{0,1:T(8,128)(2,1)} async-done(((bf16[768,768]{0,1:T(8,128)(2,1)}), bf16[768,96]{0,1:T(8,128)(2,1)}) %reduce-scatter.11.cloned.1.call-update) | async-done | bytes 147472 | tf_op jit(solution)/shard_map/reduce_scatter | solution.py:395
  (489 shorter events, 184.2 us)
Async XLA Ops:
  7.2 60.4 %all-gather.11.cloned.1.call-start = ((), (), s32[]{:S(2)}) async-start(), calls=%async_computation.10 | async-start | bytes 2359296 | tf_op jit(solution)/shard_map/all_gather | solution.py:167
  9.3 100.2 %all-gather.7.cloned.1.call-start = ((), (), s32[]{:S(2)}) async-start(), calls=%async_computation.4 | async-start | bytes 1769472 | tf_op jit(solution)/shard_map/all_gather | solution.py:218
  12.8 142.2 %all-gather.9.cloned.1.call-start = ((), (), s32[]{:S(2)}) async-start(), calls=%async_computation.5 | async-start | bytes 1769472 | tf_op jit(solution)/shard_map/all_gather | solution.py:219
  15.1 263.6 %all-reduce.6.cloned.1.call-start = ((), (), s32[]{:S(2)}) async-start(), calls=%async_computation.6 | async-start | bytes 1572864 | tf_op jit(solution)/shard_map/psum | solution.py:241
  202.3 120.3 %all-reduce.8.cloned.1.call-start = ((), (), s32[]{:S(2)}) async-start(), calls=%async_computation.7 | async-start | bytes 1572864 | tf_op jit(solution)/shard_map/psum | solution.py:270
  287.9 276.7 %reduce-scatter.15.cloned.1.call-start = ((), (), s32[]{:S(2)}) async-start(), calls=%async_computation.12 | async-start | bytes 442368
  333.2 255.1 %all-reduce.10.cloned.1.call-start = ((), (), s32[]{:S(2)}) async-start(), calls=%async_computation.13 | async-start | bytes 3145728 | tf_op jit(solution)/shard_map/psum | solution.py:254
  340.8 13.2 %collective-permute-start.4 = (bf16[512,3,64]{0,2,1:T(8,128)(2,1)}, bf16[512,3,64]{0,2,1:T(8,128)(2,1)S(1)}, u32[]{:S(2)}, u32[]{:S(2)}) collective-permute-start(bf16[512,3,64]{0,2,1:T(8,128)(2,1)} %convert_element_type.527), channel_id=1, source_target_pairs={{28,0},{0,4},{4,8},{8,12},{12,16},{16,20},{20,24},{24,28},{29,1},{... | collective-permute-start | bytes 589832 | tf_op jit(solution)/shard_map/while/body/eval_jaxpr/ppermute | solution.py:35
  342.3 13.1 %collective-permute-start.3 = (bf16[512,3,64]{0,2,1:T(8,128)(2,1)S(1)}, bf16[512,3,64]{0,2,1:T(8,128)(2,1)S(1)}, u32[]{:S(2)}, u32[]{:S(2)}) collective-permute-start(bf16[512,3,64]{0,2,1:T(8,128)(2,1)S(1)} %convert_element_type.525), channel_id=1, source_target_pairs={{28,0},{0,4},{4,8},{8,12},{12,16},{16,20},{20,24},{24,28},{29,1},{... | collective-permute-start | bytes 589832 | tf_op jit(solution)/shard_map/while/body/eval_jaxpr/ppermute | solution.py:35
  343.9 15.3 %collective-permute-start = (bf16[512,3,64]{0,2,1:T(8,128)(2,1)S(1)}, bf16[512,3,64]{0,2,1:T(8,128)(2,1)S(1)}, u32[]{:S(2)}, u32[]{:S(2)}) collective-permute-start(bf16[512,3,64]{0,2,1:T(8,128)(2,1)S(1)} %copy.153), channel_id=1, source_target_pairs={{0,4},{4,8},{8,12},{12,16},{16,20},{20,24},{24,28},{1,5},{5,9},{9,... | collective-permute-start | bytes 589832 | tf_op jit(solution)/shard_map/while/body/eval_jaxpr/ppermute | solution.py:29
  347.2 11.9 %collective-permute-start.1 = (bf16[512,3,64]{0,2,1:T(8,128)(2,1)}, bf16[512,3,64]{0,2,1:T(8,128)(2,1)}, u32[]{:S(2)}, u32[]{:S(2)}) collective-permute-start(bf16[512,3,64]{0,2,1:T(8,128)(2,1)} %copy.154), channel_id=1, source_target_pairs={{0,4},{4,8},{8,12},{12,16},{16,20},{20,24},{24,28},{1,5},{5,9},{9,... | collective-permute-start | bytes 589832 | tf_op jit(solution)/shard_map/while/body/eval_jaxpr/ppermute | solution.py:29
  351.3 7.9 collective-permute-start.2
  362.7 20.5 %collective-permute-start.4 = (bf16[512,3,64]{0,2,1:T(8,128)(2,1)}, bf16[512,3,64]{0,2,1:T(8,128)(2,1)S(1)}, u32[]{:S(2)}, u32[]{:S(2)}) collective-permute-start(bf16[512,3,64]{0,2,1:T(8,128)(2,1)} %convert_element_type.527), channel_id=1, source_target_pairs={{28,0},{0,4},{4,8},{8,12},{12,16},{16,20},{20,24},{24,28},{29,1},{... | collective-permute-start | bytes 589832 | tf_op jit(solution)/shard_map/while/body/eval_jaxpr/ppermute | solution.py:35
  370.9 13.1 %collective-permute-start.3 = (bf16[512,3,64]{0,2,1:T(8,128)(2,1)S(1)}, bf16[512,3,64]{0,2,1:T(8,128)(2,1)S(1)}, u32[]{:S(2)}, u32[]{:S(2)}) collective-permute-start(bf16[512,3,64]{0,2,1:T(8,128)(2,1)S(1)} %convert_element_type.525), channel_id=1, source_target_pairs={{28,0},{0,4},{4,8},{8,12},{12,16},{16,20},{20,24},{24,28},{29,1},{... | collective-permute-start | bytes 589832 | tf_op jit(solution)/shard_map/while/body/eval_jaxpr/ppermute | solution.py:35
  374.4 12.8 %collective-permute-start = (bf16[512,3,64]{0,2,1:T(8,128)(2,1)S(1)}, bf16[512,3,64]{0,2,1:T(8,128)(2,1)S(1)}, u32[]{:S(2)}, u32[]{:S(2)}) collective-permute-start(bf16[512,3,64]{0,2,1:T(8,128)(2,1)S(1)} %copy.153), channel_id=1, source_target_pairs={{0,4},{4,8},{8,12},{12,16},{16,20},{20,24},{24,28},{1,5},{5,9},{9,... | collective-permute-start | bytes 589832 | tf_op jit(solution)/shard_map/while/body/eval_jaxpr/ppermute | solution.py:29
  376.3 10.8 %collective-permute-start.1 = (bf16[512,3,64]{0,2,1:T(8,128)(2,1)}, bf16[512,3,64]{0,2,1:T(8,128)(2,1)}, u32[]{:S(2)}, u32[]{:S(2)}) collective-permute-start(bf16[512,3,64]{0,2,1:T(8,128)(2,1)} %copy.154), channel_id=1, source_target_pairs={{0,4},{4,8},{8,12},{12,16},{16,20},{20,24},{24,28},{1,5},{5,9},{9,... | collective-permute-start | bytes 589832 | tf_op jit(solution)/shard_map/while/body/eval_jaxpr/ppermute | solution.py:29
  381.9 5.2 collective-permute-start.2
  390.7 19.4 %collective-permute-start.4 = (bf16[512,3,64]{0,2,1:T(8,128)(2,1)}, bf16[512,3,64]{0,2,1:T(8,128)(2,1)S(1)}, u32[]{:S(2)}, u32[]{:S(2)}) collective-permute-start(bf16[512,3,64]{0,2,1:T(8,128)(2,1)} %convert_element_type.527), channel_id=1, source_target_pairs={{28,0},{0,4},{4,8},{8,12},{12,16},{16,20},{20,24},{24,28},{29,1},{... | collective-permute-start | bytes 589832 | tf_op jit(solution)/shard_map/while/body/eval_jaxpr/ppermute | solution.py:35
  393.2 17.7 %collective-permute-start.3 = (bf16[512,3,64]{0,2,1:T(8,128)(2,1)S(1)}, bf16[512,3,64]{0,2,1:T(8,128)(2,1)S(1)}, u32[]{:S(2)}, u32[]{:S(2)}) collective-permute-start(bf16[512,3,64]{0,2,1:T(8,128)(2,1)S(1)} %convert_element_type.525), channel_id=1, source_target_pairs={{28,0},{0,4},{4,8},{8,12},{12,16},{16,20},{20,24},{24,28},{29,1},{... | collective-permute-start | bytes 589832 | tf_op jit(solution)/shard_map/while/body/eval_jaxpr/ppermute | solution.py:35
  401.5 10.3 %collective-permute-start = (bf16[512,3,64]{0,2,1:T(8,128)(2,1)S(1)}, bf16[512,3,64]{0,2,1:T(8,128)(2,1)S(1)}, u32[]{:S(2)}, u32[]{:S(2)}) collective-permute-start(bf16[512,3,64]{0,2,1:T(8,128)(2,1)S(1)} %copy.153), channel_id=1, source_target_pairs={{0,4},{4,8},{8,12},{12,16},{16,20},{20,24},{24,28},{1,5},{5,9},{9,... | collective-permute-start | bytes 589832 | tf_op jit(solution)/shard_map/while/body/eval_jaxpr/ppermute | solution.py:29
  403.4 8.4 %collective-permute-start.1 = (bf16[512,3,64]{0,2,1:T(8,128)(2,1)}, bf16[512,3,64]{0,2,1:T(8,128)(2,1)}, u32[]{:S(2)}, u32[]{:S(2)}) collective-permute-start(bf16[512,3,64]{0,2,1:T(8,128)(2,1)} %copy.154), channel_id=1, source_target_pairs={{0,4},{4,8},{8,12},{12,16},{16,20},{20,24},{24,28},{1,5},{5,9},{9,... | collective-permute-start | bytes 589832 | tf_op jit(solution)/shard_map/while/body/eval_jaxpr/ppermute | solution.py:29
  408.9 2.9 collective-permute-start.2
  415.4 22.2 %collective-permute-start.4 = (bf16[512,3,64]{0,2,1:T(8,128)(2,1)}, bf16[512,3,64]{0,2,1:T(8,128)(2,1)S(1)}, u32[]{:S(2)}, u32[]{:S(2)}) collective-permute-start(bf16[512,3,64]{0,2,1:T(8,128)(2,1)} %convert_element_type.527), channel_id=1, source_target_pairs={{28,0},{0,4},{4,8},{8,12},{12,16},{16,20},{20,24},{24,28},{29,1},{... | collective-permute-start | bytes 589832 | tf_op jit(solution)/shard_map/while/body/eval_jaxpr/ppermute | solution.py:35
  420.8 17.6 %collective-permute-start.3 = (bf16[512,3,64]{0,2,1:T(8,128)(2,1)S(1)}, bf16[512,3,64]{0,2,1:T(8,128)(2,1)S(1)}, u32[]{:S(2)}, u32[]{:S(2)}) collective-permute-start(bf16[512,3,64]{0,2,1:T(8,128)(2,1)S(1)} %convert_element_type.525), channel_id=1, source_target_pairs={{28,0},{0,4},{4,8},{8,12},{12,16},{16,20},{20,24},{24,28},{29,1},{... | collective-permute-start | bytes 589832 | tf_op jit(solution)/shard_map/while/body/eval_jaxpr/ppermute | solution.py:35
  424.2 15.0 %collective-permute-start = (bf16[512,3,64]{0,2,1:T(8,128)(2,1)S(1)}, bf16[512,3,64]{0,2,1:T(8,128)(2,1)S(1)}, u32[]{:S(2)}, u32[]{:S(2)}) collective-permute-start(bf16[512,3,64]{0,2,1:T(8,128)(2,1)S(1)} %copy.153), channel_id=1, source_target_pairs={{0,4},{4,8},{8,12},{12,16},{16,20},{20,24},{24,28},{1,5},{5,9},{9,... | collective-permute-start | bytes 589832 | tf_op jit(solution)/shard_map/while/body/eval_jaxpr/ppermute | solution.py:29
  430.3 8.9 %collective-permute-start.1 = (bf16[512,3,64]{0,2,1:T(8,128)(2,1)}, bf16[512,3,64]{0,2,1:T(8,128)(2,1)}, u32[]{:S(2)}, u32[]{:S(2)}) collective-permute-start(bf16[512,3,64]{0,2,1:T(8,128)(2,1)} %copy.154), channel_id=1, source_target_pairs={{0,4},{4,8},{8,12},{12,16},{16,20},{20,24},{24,28},{1,5},{5,9},{9,... | collective-permute-start | bytes 589832 | tf_op jit(solution)/shard_map/while/body/eval_jaxpr/ppermute | solution.py:29
  442.8 20.4 %collective-permute-start.4 = (bf16[512,3,64]{0,2,1:T(8,128)(2,1)}, bf16[512,3,64]{0,2,1:T(8,128)(2,1)S(1)}, u32[]{:S(2)}, u32[]{:S(2)}) collective-permute-start(bf16[512,3,64]{0,2,1:T(8,128)(2,1)} %convert_element_type.527), channel_id=1, source_target_pairs={{28,0},{0,4},{4,8},{8,12},{12,16},{16,20},{20,24},{24,28},{29,1},{... | collective-permute-start | bytes 589832 | tf_op jit(solution)/shard_map/while/body/eval_jaxpr/ppermute | solution.py:35
  445.8 18.2 %collective-permute-start.3 = (bf16[512,3,64]{0,2,1:T(8,128)(2,1)S(1)}, bf16[512,3,64]{0,2,1:T(8,128)(2,1)S(1)}, u32[]{:S(2)}, u32[]{:S(2)}) collective-permute-start(bf16[512,3,64]{0,2,1:T(8,128)(2,1)S(1)} %convert_element_type.525), channel_id=1, source_target_pairs={{28,0},{0,4},{4,8},{8,12},{12,16},{16,20},{20,24},{24,28},{29,1},{... | collective-permute-start | bytes 589832 | tf_op jit(solution)/shard_map/while/body/eval_jaxpr/ppermute | solution.py:35
  448.7 16.2 %collective-permute-start = (bf16[512,3,64]{0,2,1:T(8,128)(2,1)S(1)}, bf16[512,3,64]{0,2,1:T(8,128)(2,1)S(1)}, u32[]{:S(2)}, u32[]{:S(2)}) collective-permute-start(bf16[512,3,64]{0,2,1:T(8,128)(2,1)S(1)} %copy.153), channel_id=1, source_target_pairs={{0,4},{4,8},{8,12},{12,16},{16,20},{20,24},{24,28},{1,5},{5,9},{9,... | collective-permute-start | bytes 589832 | tf_op jit(solution)/shard_map/while/body/eval_jaxpr/ppermute | solution.py:29
  451.2 13.7 %collective-permute-start.1 = (bf16[512,3,64]{0,2,1:T(8,128)(2,1)}, bf16[512,3,64]{0,2,1:T(8,128)(2,1)}, u32[]{:S(2)}, u32[]{:S(2)}) collective-permute-start(bf16[512,3,64]{0,2,1:T(8,128)(2,1)} %copy.154), channel_id=1, source_target_pairs={{0,4},{4,8},{8,12},{12,16},{16,20},{20,24},{24,28},{1,5},{5,9},{9,... | collective-permute-start | bytes 589832 | tf_op jit(solution)/shard_map/while/body/eval_jaxpr/ppermute | solution.py:29
  468.5 18.9 %collective-permute-start.4 = (bf16[512,3,64]{0,2,1:T(8,128)(2,1)}, bf16[512,3,64]{0,2,1:T(8,128)(2,1)S(1)}, u32[]{:S(2)}, u32[]{:S(2)}) collective-permute-start(bf16[512,3,64]{0,2,1:T(8,128)(2,1)} %convert_element_type.527), channel_id=1, source_target_pairs={{28,0},{0,4},{4,8},{8,12},{12,16},{16,20},{20,24},{24,28},{29,1},{... | collective-permute-start | bytes 589832 | tf_op jit(solution)/shard_map/while/body/eval_jaxpr/ppermute | solution.py:35
  471.4 16.8 %collective-permute-start.3 = (bf16[512,3,64]{0,2,1:T(8,128)(2,1)S(1)}, bf16[512,3,64]{0,2,1:T(8,128)(2,1)S(1)}, u32[]{:S(2)}, u32[]{:S(2)}) collective-permute-start(bf16[512,3,64]{0,2,1:T(8,128)(2,1)S(1)} %convert_element_type.525), channel_id=1, source_target_pairs={{28,0},{0,4},{4,8},{8,12},{12,16},{16,20},{20,24},{24,28},{29,1},{... | collective-permute-start | bytes 589832 | tf_op jit(solution)/shard_map/while/body/eval_jaxpr/ppermute | solution.py:35
  474.3 14.7 %collective-permute-start = (bf16[512,3,64]{0,2,1:T(8,128)(2,1)S(1)}, bf16[512,3,64]{0,2,1:T(8,128)(2,1)S(1)}, u32[]{:S(2)}, u32[]{:S(2)}) collective-permute-start(bf16[512,3,64]{0,2,1:T(8,128)(2,1)S(1)} %copy.153), channel_id=1, source_target_pairs={{0,4},{4,8},{8,12},{12,16},{16,20},{20,24},{24,28},{1,5},{5,9},{9,... | collective-permute-start | bytes 589832 | tf_op jit(solution)/shard_map/while/body/eval_jaxpr/ppermute | solution.py:29
  476.2 12.8 %collective-permute-start.1 = (bf16[512,3,64]{0,2,1:T(8,128)(2,1)}, bf16[512,3,64]{0,2,1:T(8,128)(2,1)}, u32[]{:S(2)}, u32[]{:S(2)}) collective-permute-start(bf16[512,3,64]{0,2,1:T(8,128)(2,1)} %copy.154), channel_id=1, source_target_pairs={{0,4},{4,8},{8,12},{12,16},{16,20},{20,24},{24,28},{1,5},{5,9},{9,... | collective-permute-start | bytes 589832 | tf_op jit(solution)/shard_map/while/body/eval_jaxpr/ppermute | solution.py:29
  481.9 7.1 collective-permute-start.2
  492.6 13.6 %collective-permute-start.4 = (bf16[512,3,64]{0,2,1:T(8,128)(2,1)}, bf16[512,3,64]{0,2,1:T(8,128)(2,1)S(1)}, u32[]{:S(2)}, u32[]{:S(2)}) collective-permute-start(bf16[512,3,64]{0,2,1:T(8,128)(2,1)} %convert_element_type.527), channel_id=1, source_target_pairs={{28,0},{0,4},{4,8},{8,12},{12,16},{16,20},{20,24},{24,28},{29,1},{... | collective-permute-start | bytes 589832 | tf_op jit(solution)/shard_map/while/body/eval_jaxpr/ppermute | solution.py:35
  496.1 11.8 %collective-permute-start.3 = (bf16[512,3,64]{0,2,1:T(8,128)(2,1)S(1)}, bf16[512,3,64]{0,2,1:T(8,128)(2,1)S(1)}, u32[]{:S(2)}, u32[]{:S(2)}) collective-permute-start(bf16[512,3,64]{0,2,1:T(8,128)(2,1)S(1)} %convert_element_type.525), channel_id=1, source_target_pairs={{28,0},{0,4},{4,8},{8,12},{12,16},{16,20},{20,24},{24,28},{29,1},{... | collective-permute-start | bytes 589832 | tf_op jit(solution)/shard_map/while/body/eval_jaxpr/ppermute | solution.py:35
  498.9 9.7 %collective-permute-start = (bf16[512,3,64]{0,2,1:T(8,128)(2,1)S(1)}, bf16[512,3,64]{0,2,1:T(8,128)(2,1)S(1)}, u32[]{:S(2)}, u32[]{:S(2)}) collective-permute-start(bf16[512,3,64]{0,2,1:T(8,128)(2,1)S(1)} %copy.153), channel_id=1, source_target_pairs={{0,4},{4,8},{8,12},{12,16},{16,20},{20,24},{24,28},{1,5},{5,9},{9,... | collective-permute-start | bytes 589832 | tf_op jit(solution)/shard_map/while/body/eval_jaxpr/ppermute | solution.py:29
  500.9 7.8 collective-permute-start.1
  503.9 4.7 collective-permute-start.2
  512.3 16.6 %collective-permute-start.4 = (bf16[512,3,64]{0,2,1:T(8,128)(2,1)}, bf16[512,3,64]{0,2,1:T(8,128)(2,1)S(1)}, u32[]{:S(2)}, u32[]{:S(2)}) collective-permute-start(bf16[512,3,64]{0,2,1:T(8,128)(2,1)} %convert_element_type.527), channel_id=1, source_target_pairs={{28,0},{0,4},{4,8},{8,12},{12,16},{16,20},{20,24},{24,28},{29,1},{... | collective-permute-start | bytes 589832 | tf_op jit(solution)/shard_map/while/body/eval_jaxpr/ppermute | solution.py:35
  519.7 10.8 %collective-permute-start.3 = (bf16[512,3,64]{0,2,1:T(8,128)(2,1)S(1)}, bf16[512,3,64]{0,2,1:T(8,128)(2,1)S(1)}, u32[]{:S(2)}, u32[]{:S(2)}) collective-permute-start(bf16[512,3,64]{0,2,1:T(8,128)(2,1)S(1)} %convert_element_type.525), channel_id=1, source_target_pairs={{28,0},{0,4},{4,8},{8,12},{12,16},{16,20},{20,24},{24,28},{29,1},{... | collective-permute-start | bytes 589832 | tf_op jit(solution)/shard_map/while/body/eval_jaxpr/ppermute | solution.py:35
  522.5 8.7 %collective-permute-start = (bf16[512,3,64]{0,2,1:T(8,128)(2,1)S(1)}, bf16[512,3,64]{0,2,1:T(8,128)(2,1)S(1)}, u32[]{:S(2)}, u32[]{:S(2)}) collective-permute-start(bf16[512,3,64]{0,2,1:T(8,128)(2,1)S(1)} %copy.153), channel_id=1, source_target_pairs={{0,4},{4,8},{8,12},{12,16},{16,20},{20,24},{24,28},{1,5},{5,9},{9,... | collective-permute-start | bytes 589832 | tf_op jit(solution)/shard_map/while/body/eval_jaxpr/ppermute | solution.py:29
  525.0 6.3 collective-permute-start.1
  527.6 3.7 collective-permute-start.2
  540.7 114.6 %reduce-scatter.13.cloned.1.call-start = ((), (), s32[]{:S(2)}) async-start(), calls=%async_computation.11 | async-start | bytes 1105920
  547.3 175.0 %reduce-scatter.9.cloned.1.call-start = ((), (), s32[]{:S(2)}) async-start(), calls=%async_computation.8 | async-start | bytes 1327104 | tf_op jit(solution)/shard_map/reduce_scatter | solution.py:394
  550.7 238.4 %reduce-scatter.11.cloned.1.call-start = ((), (), s32[]{:S(2)}) async-start(), calls=%async_computation.9 | async-start | bytes 1327104 | tf_op jit(solution)/shard_map/reduce_scatter | solution.py:395
  (94 other events, 913.8 us)
Sparse Core Ops, SparseCore 0:
  10.8 52.1 all-gather.10
  65.6 43.8 all-gather.6
  111.5 43.4 all-gather.8
  202.5 76.2 all-reduce.5
  288.0 34.6 all-reduce.7
  333.3 77.1 reduce-scatter.14
  540.8 47.4 all-reduce.9
  591.6 63.5 reduce-scatter.12
  659.0 63.2 reduce-scatter.8
  725.9 63.1 reduce-scatter.10

commit v2 on v1

--- a/solution.py
+++ b/solution.py
@@ -1,4 +1,4 @@
-import math
+import functools
 
 import ml_dtypes
 import numpy as np
@@ -6,6 +6,8 @@
 import jax
 import jax.numpy as jnp
 from jax import lax
+from jax.experimental import pallas as pl
+from jax.experimental.pallas import tpu as pltpu
 from jax.sharding import PartitionSpec as P
 
 D = 768
@@ -21,18 +23,8 @@
 SPREAD = 0.01
 NEGATIVE = -1e30
 UPPER_LIMIT = lax.Precision.HIGHEST
-
-
-def shifted(block, axis, distance):
-    devices = range(lax.axis_size(axis))
-    route = [(i - distance, i) for i in devices if i - distance in devices]
-    return lax.ppermute(block, axis, route)
-
-
-def passed_along(block, axis, distance):
-    devices = range(lax.axis_size(axis))
-    route = [((i - distance) % len(devices), i) for i in devices]
-    return lax.ppermute(block, axis, route)
+MESH_ID = pl.DeviceIdType.MESH
+VMEM_LIMIT = 60 * 2**20
 
 
 def layer_norm(rows_in, gain_vec, bias_vec):
@@ -72,60 +64,605 @@
     return high, lower
 
 
-def block_rows(row_count_total, tok_rows):
-    return math.gcd(row_count_total, max(512, tok_rows))
-
-
-def split_blocks(array_in, blk_rows):
-    blk_count = array_in.shape[0] // blk_rows
-    return array_in.reshape((blk_count, blk_rows) + array_in.shape[1:])
-
-
-def keep_state(running):
-    return running
-
-
-def forward_folder(queries, own_pos, own_doc, scale_dh, fold_state, shard_piece):
-    key_part, val_part, doc_part = shard_piece
-    blk_rows = block_rows(key_part.shape[0], queries.shape[0])
-    blk_count = key_part.shape[0] // blk_rows
-
-    def one_block(running, block_item):
-        key_blk, val_blk, doc_blk, blk_index = block_item
-        key_pos = blk_index * blk_rows + jnp.arange(blk_rows, dtype=jnp.int32)
-
-        def one_compute(current):
-            row_max, row_sum, accumulated = current
-            visible = (
-                (own_pos[:, None] >= key_pos[None, :]) & (own_doc[:, None] == doc_blk[None, :])
-            )[:, None, :]
-            scores = (
-                jnp.einsum("qhd,khd->qhk", queries, key_blk, preferred_element_type=jnp.float32)
-                * scale_dh
+LANES_OUT = 256
+
+
+def head_of_lane(width):
+    return lax.broadcasted_iota(jnp.int32, (1, width), 1) // DH
+
+
+def head_masks(width):
+    lane_head = head_of_lane(width)
+    return [(lane_head == head).astype(jnp.float32).astype(jnp.bfloat16) for head in range(width // DH)]
+
+
+def pick_heads(per_head, lane_head):
+    chosen = per_head[0]
+    for head in range(1, len(per_head)):
+        chosen = jnp.where(lane_head == head, per_head[head], chosen)
+    return chosen
+
+
+def dot_rows(left, right):
+    return lax.dot_general(left, right, (((1,), (1,)), ((), ())), preferred_element_type=jnp.float32)
+
+
+def dot_plain(left, right):
+    return lax.dot_general(left, right, (((1,), (0,)), ((), ())), preferred_element_type=jnp.float32)
+
+
+def thirds(value):
+    first = value.astype(jnp.bfloat16)
+    rest = value - first.astype(jnp.float32)
+    second = rest.astype(jnp.bfloat16)
+    third = (rest - second.astype(jnp.float32)).astype(jnp.bfloat16)
+    return first, second, third
+
+
+def with_stats(block, stats):
+    rows, width = block.shape
+    spare = LANES_OUT - width
+    lane = lax.broadcasted_iota(jnp.int32, (1, spare), 1)
+    tail = jnp.zeros((rows, spare), jnp.float32)
+    for index, column in enumerate(stats):
+        for part, value in enumerate(thirds(column)):
+            tail = jnp.where(lane == 3 * index + part, value.astype(jnp.float32), tail)
+    return jnp.concatenate([block, tail.astype(jnp.bfloat16)], axis=1)
+
+
+def stat_column(extended, width, index):
+    lane = lax.broadcasted_iota(jnp.int32, (1, LANES_OUT), 1)
+    start = width + 3 * index
+    mine = (lane >= start) & (lane < start + 3)
+    return jnp.sum(jnp.where(mine, extended.astype(jnp.float32), 0.0), axis=1, keepdims=True)
+
+
+def stat_rows(extended, width, count):
+    row = lax.broadcasted_iota(jnp.int32, (count, LANES_OUT), 0)
+    lane = lax.broadcasted_iota(jnp.int32, (count, LANES_OUT), 1)
+    start = width + 3 * row
+    chooser = ((lane >= start) & (lane < start + 3)).astype(jnp.float32).astype(jnp.bfloat16)
+    return dot_rows(chooser, extended)
+
+
+def greet(levels):
+    seq, tp = lax.axis_index("seq"), lax.axis_index("tp")
+    level, side = seq // 2, seq % 2
+    barrier = pltpu.get_barrier_semaphore()
+    pl.semaphore_signal(barrier, inc=1, device_id=(2 * level + 1 - side, tp), device_id_type=MESH_ID)
+
+    def one(step, unused):
+        other = lax.rem(level + step, levels)
+        pl.semaphore_signal(barrier, inc=1, device_id=(2 * other + side, tp), device_id_type=MESH_ID)
+        return unused
+
+    lax.fori_loop(1, levels, one, 0)
+    return barrier, levels
+
+
+def forward_kernel(
+    levels,
+    tok_ref,
+    norm_ref,
+    weight_ref,
+    bias_ref,
+    doc_col_ref,
+    doc_row_ref,
+    key_mask_ref,
+    normed_ref,
+    query_out_ref,
+    kv_out_ref,
+    out_ref,
+    lse_ref,
+    pair_ref,
+    top_ref,
+    total_ref,
+    acc_ref,
+    part_ref,
+    part_in_ref,
+    kv_send,
+    kv_recv,
+    q_send,
+    q_recv,
+    pair_sem,
+    part_sem,
+):
+    seq, tp = lax.axis_index("seq"), lax.axis_index("tp")
+    level, side = seq // 2, seq % 2
+    rows = tok_ref.shape[0]
+    width = pair_ref.shape[2]
+    heads = width // DH
+    partner = (2 * level + 1 - side, tp)
+    lane_head = head_of_lane(width)
+    head_mask = head_masks(width)
+    barrier, greetings = greet(levels)
+
+    chunk = rows // 2
+
+    def project(index, unused):
+        here = pl.ds(pl.multiple_of(index * chunk, chunk), chunk)
+        x = tok_ref[here, :].astype(jnp.float32)
+        centred = x - jnp.mean(x, axis=1, keepdims=True)
+        variance = jnp.mean(centred * centred, axis=1, keepdims=True)
+        a = centred * lax.rsqrt(variance + EPS) * norm_ref[0:1, :] + norm_ref[1:2, :]
+        a = a.astype(jnp.bfloat16)
+        normed_ref[here, :] = a
+        mixed = (dot_plain(a, weight_ref[...]) + bias_ref[0:1, :]).astype(jnp.bfloat16)
+        query = mixed[:, :width] * jnp.bfloat16(DH**-0.5)
+        pair_ref[0, here, :] = query
+        query_out_ref[level, here, :] = query
+        kv_out_ref[level, here, :] = mixed[:, width:]
+        return unused
+
+    lax.fori_loop(0, rows // chunk, project, 0)
+    kv_out_ref[level, rows:, :] = key_mask_ref[...]
+
+    pl.semaphore_wait(barrier, greetings)
+    pair_copy = pltpu.make_async_remote_copy(
+        pair_ref.at[0], pair_ref.at[1], pair_sem.at[0], pair_sem.at[1], device_id=partner, device_id_type=MESH_ID
+    )
+    pair_copy.start()
+
+    def kv_copy(from_level):
+        return pltpu.make_async_remote_copy(
+            kv_out_ref.at[from_level],
+            kv_out_ref.at[from_level],
+            kv_send.at[from_level],
+            kv_recv.at[from_level],
+            device_id=(lax.rem(2 * level + 2, 2 * levels) + side, tp),
+            device_id_type=MESH_ID,
+        )
+
+    def query_copy(from_level, to_level):
+        return pltpu.make_async_remote_copy(
+            query_out_ref.at[from_level],
+            query_out_ref.at[from_level],
+            q_send.at[to_level],
+            q_recv.at[from_level],
+            device_id=(2 * to_level + side, tp),
+            device_id_type=MESH_ID,
+        )
+
+    @pl.when(level < levels - 1)
+    def _():
+        kv_copy(level).start()
+
+    def send_down(step, unused):
+        query_copy(level, level - step).start()
+        return unused
+
+    lax.fori_loop(1, level + 1, send_down, 0)
+
+    top_ref[...] = jnp.full(top_ref.shape, NEGATIVE, jnp.float32)
+    total_ref[...] = jnp.zeros(total_ref.shape, jnp.float32)
+    acc_ref[...] = jnp.zeros(acc_ref.shape, jnp.float32)
+
+    doc_first = doc_row_ref[0:1, 0:1]
+    def reach_of(here):
+        docs = doc_col_ref[here, :]
+        last = (level == levels - 1) & (side == 1)
+        return jnp.where(last & (docs != doc_first), NEGATIVE, 0.0)
+
+    def fold(slot, from_level, mask_kind):
+        mask_rows = kv_out_ref[from_level, rows:, :].astype(jnp.float32)
+        key_mask = jnp.concatenate([mask_rows[0:1, : rows // 2], mask_rows[1:2, : rows // 2]], axis=1)
+
+        def part(index, unused):
+            here = pl.ds(pl.multiple_of(index * chunk, chunk), chunk)
+            query = pair_ref[slot, here, :]
+            keys = kv_out_ref[from_level, :rows, :width]
+            vals = kv_out_ref[from_level, :rows, width:]
+            if mask_kind == "own":
+                q_pos = index * chunk + lax.broadcasted_iota(jnp.int32, (chunk, rows), 0)
+                k_pos = lax.broadcasted_iota(jnp.int32, (chunk, rows), 1)
+                visible = (q_pos >= k_pos) & (doc_col_ref[here, :] == doc_row_ref[0:1, :])
+            products, scales = [], []
+            for head in range(heads):
+                scores = dot_rows(query * head_mask[head], keys)
+                old_top = top_ref[slot, head, here, :]
+                if mask_kind == "own":
+                    scores = jnp.where(visible, scores, NEGATIVE)
+                    reach = 0.0
+                else:
+                    scores = scores + key_mask
+                    reach = jnp.where(slot == 0, reach_of(here), 0.0)
+                new_top = jnp.maximum(old_top, jnp.max(scores, axis=1, keepdims=True) + reach)
+                weights = jnp.exp(scores - (new_top - reach))
+                scale = jnp.exp(old_top - new_top)
+                top_ref[slot, head, here, :] = new_top
+                total_ref[slot, head, here, :] = total_ref[slot, head, here, :] * scale + jnp.sum(
+                    weights, axis=1, keepdims=True
+                )
+                products.append(dot_plain(weights.astype(jnp.bfloat16), vals))
+                scales.append(scale)
+            acc_ref[slot, here, :] = acc_ref[slot, here, :] * pick_heads(scales, lane_head) + pick_heads(
+                products, lane_head
             )
-            scores = jnp.where(visible, scores, NEGATIVE)
-            new_max = jnp.maximum(row_max, jnp.max(scores, axis=-1))
-            exp_vals = jnp.where(visible, jnp.exp(scores - new_max[..., None]), 0.0)
-            adjustment_term = jnp.exp(row_max - new_max)
-            new_sum = row_sum * adjustment_term + jnp.sum(exp_vals, axis=-1)
-            new_acc = accumulated * adjustment_term[..., None] + jnp.einsum(
-                "qhk,khd->qhd",
-                exp_vals.astype(jnp.bfloat16),
-                val_blk,
-                preferred_element_type=jnp.float32,
+            return unused
+
+        lax.fori_loop(0, rows // chunk, part, 0)
+
+    fold(0, level, "own")
+    pair_copy.wait()
+
+    @pl.when(side == 0)
+    def _():
+        fold(1, level, "off")
+
+    def arrived(step, unused):
+        from_level = level - step
+        kv_copy(from_level).wait_recv()
+
+        @pl.when(level < levels - 1)
+        def _():
+            kv_copy(from_level).start()
+
+        def both(slot, inner):
+            fold(slot, from_level, "off")
+            return inner
+
+        lax.fori_loop(0, 2, both, 0)
+        return unused
+
+    lax.fori_loop(1, level + 1, arrived, 0)
+
+    def finish(index, unused):
+        here = pl.ds(pl.multiple_of(index * chunk, chunk), chunk)
+        totals = [total_ref[1, head, here, :] for head in range(heads)]
+        tops = [top_ref[1, head, here, :] for head in range(heads)]
+        some = [value > 0.0 for value in totals]
+        inverse = [jnp.where(ok, 1.0 / jnp.where(ok, value, 1.0), 0.0) for ok, value in zip(some, totals)]
+        logs = [
+            jnp.where(ok, top + jnp.log(jnp.where(ok, value, 1.0)), NEGATIVE)
+            for ok, top, value in zip(some, tops, totals)
+        ]
+        share = (acc_ref[1, here, :] * pick_heads(inverse, lane_head)).astype(jnp.bfloat16)
+        part_ref[here, :] = with_stats(share, logs)
+        return unused
+
+    lax.fori_loop(0, rows // chunk, finish, 0)
+    part_copy = pltpu.make_async_remote_copy(
+        part_ref, part_in_ref, part_sem.at[0], part_sem.at[1], device_id=partner, device_id_type=MESH_ID
+    )
+    part_copy.start()
+    part_copy.wait()
+
+    def merge(index, unused):
+        here = pl.ds(pl.multiple_of(index * chunk, chunk), chunk)
+        reach = reach_of(here)
+        received = part_in_ref[here, :]
+        mine, theirs, columns = [], [], []
+        for head in range(heads):
+            total = total_ref[0, head, here, :]
+            own_log = top_ref[0, head, here, :] + jnp.log(total)
+            other_log = stat_column(received, width, head) + reach
+            high = jnp.maximum(own_log, other_log)
+            both_log = high + jnp.log(jnp.exp(own_log - high) + jnp.exp(other_log - high))
+            mine.append(jnp.exp(own_log - both_log) / total)
+            theirs.append(jnp.exp(other_log - both_log))
+            columns.append(both_log)
+        out_ref[here, :] = acc_ref[0, here, :] * pick_heads(mine, lane_head) + received[
+            :, :width
+        ].astype(jnp.float32) * pick_heads(theirs, lane_head)
+        lane = lax.broadcasted_iota(jnp.int32, (1, 8), 1)
+        packed = jnp.zeros((chunk, 8), jnp.float32)
+        for head in range(heads):
+            packed = jnp.where(lane == head, columns[head], packed)
+        lse_ref[here, :] = packed
+        return unused
+
+    lax.fori_loop(0, rows // chunk, merge, 0)
+
+    def sent_down(step, unused):
+        query_copy(level, level - step).wait_send()
+        return unused
+
+    lax.fori_loop(1, level + 1, sent_down, 0)
+
+    def from_above(step, unused):
+        query_copy(level + step, level).wait_recv()
+        return unused
+
+    lax.fori_loop(1, levels - level, from_above, 0)
+
+    @pl.when(level < levels - 1)
+    def _():
+        def sent_up(from_level, unused):
+            kv_copy(from_level).wait_send()
+            return unused
+
+        lax.fori_loop(0, level + 1, sent_up, 0)
+
+
+def attention_forward(levels, tokens, norm, weight, bias, doc_ids, key_mask):
+    rows = tokens.shape[0]
+    width = weight.shape[1] // 3
+    heads = width // DH
+    vmem = pl.BlockSpec(memory_space=pltpu.VMEM)
+    dma = pltpu.SemaphoreType.DMA
+    return pl.pallas_call(
+        functools.partial(forward_kernel, levels),
+        out_shape=(
+            jax.ShapeDtypeStruct((rows, D), jnp.bfloat16),
+            jax.ShapeDtypeStruct((levels, rows, width), jnp.bfloat16),
+            jax.ShapeDtypeStruct((levels, rows + 16, 2 * width), jnp.bfloat16),
+            jax.ShapeDtypeStruct((rows, width), jnp.float32),
+            jax.ShapeDtypeStruct((rows, 8), jnp.float32),
+        ),
+        in_specs=[vmem] * 7,
+        out_specs=(vmem,) * 5,
+        scratch_shapes=[
+            pltpu.VMEM((2, rows, width), jnp.bfloat16),
+            pltpu.VMEM((2, heads, rows, 1), jnp.float32),
+            pltpu.VMEM((2, heads, rows, 1), jnp.float32),
+            pltpu.VMEM((2, rows, width), jnp.float32),
+            pltpu.VMEM((rows, LANES_OUT), jnp.bfloat16),
+            pltpu.VMEM((rows, LANES_OUT), jnp.bfloat16),
+            dma((levels,)),
+            dma((levels,)),
+            dma((levels,)),
+            dma((levels,)),
+            dma((2,)),
+            dma((2,)),
+        ],
+        name="attention_forward",
+        compiler_params=pltpu.CompilerParams(
+            collective_id=1, has_side_effects=True, vmem_limit_bytes=VMEM_LIMIT
+        ),
+    )(tokens, norm, weight, bias, doc_ids[:, None], doc_ids[None, :], key_mask)
+
+
+def backward_kernel(
+    levels,
+    grad_ref,
+    attended_ref,
+    lse_ref,
+    query_col_ref,
+    query_oth_ref,
+    kv_col_ref,
+    kv_oth_ref,
+    doc_col_ref,
+    doc_row_ref,
+    dq_ref,
+    dk_ref,
+    dv_ref,
+    own_ref,
+    grad_col_ref,
+    grad_oth_ref,
+    stat_ref,
+    col_send,
+    col_recv,
+    oth_send,
+    oth_recv,
+    *staging,
+):
+    seq, tp = lax.axis_index("seq"), lax.axis_index("tp")
+    level, side = seq // 2, seq % 2
+    rows, width = grad_ref.shape
+    heads = width // DH
+    partner = (2 * level + 1 - side, tp)
+    lane_head = head_of_lane(width)
+    head_mask = head_masks(width)
+    chunk = rows // 2
+    barrier, greetings = greet(levels)
+    doc_first = doc_row_ref[0:1, 0:1]
+    last = (level == levels - 1) & (side == 1)
+
+    def prepare(index, unused):
+        here = pl.ds(pl.multiple_of(index * chunk, chunk), chunk)
+        grad = grad_ref[here, :]
+        product = grad.astype(jnp.float32) * attended_ref[here, :]
+        far = jnp.where(last & (doc_col_ref[here, :] != doc_first), -NEGATIVE, 0.0)
+        lses = [lse_ref[here, head : head + 1] for head in range(heads)]
+        deltas = [
+            jnp.sum(jnp.where(lane_head == head, product, 0.0), axis=1, keepdims=True)
+            for head in range(heads)
+        ]
+        own_ref[here, :] = with_stats(grad, lses + deltas)
+        grad_col_ref[level, here, :] = with_stats(grad, [lse + far for lse in lses] + deltas)
+        for head in range(heads):
+            stat_ref[head, here, :] = lses[head]
+            stat_ref[heads + head, here, :] = lses[head] + far
+            stat_ref[2 * heads + head, here, :] = deltas[head]
+        return unused
+
+    lax.fori_loop(0, rows // chunk, prepare, 0)
+    pl.semaphore_wait(barrier, greetings)
+
+    def col_copy(from_level, to_level):
+        return pltpu.make_async_remote_copy(
+            grad_col_ref.at[from_level],
+            grad_col_ref.at[from_level],
+            col_send.at[to_level],
+            col_recv.at[from_level],
+            device_id=(2 * to_level + side, tp),
+            device_id_type=MESH_ID,
+        )
+
+    def oth_copy(from_level):
+        return pltpu.make_async_remote_copy(
+            grad_col_ref.at[from_level],
+            grad_oth_ref.at[from_level],
+            oth_send.at[from_level],
+            oth_recv.at[from_level],
+            device_id=partner,
+            device_id_type=MESH_ID,
+        )
+
+    @pl.when(side == 1)
+    def _():
+        oth_copy(level).start()
+
+    def send_down(step, unused):
+        col_copy(level, level - step).start()
+        return unused
+
+    lax.fori_loop(1, level + 1, send_down, 0)
+
+    dq_ref[...] = jnp.zeros(dq_ref.shape, jnp.float32)
+    dk_ref[...] = jnp.zeros(dk_ref.shape, jnp.float32)
+    dv_ref[...] = jnp.zeros(dv_ref.shape, jnp.float32)
+
+    def block_of(kv_ref, from_level):
+        if not staging:
+            return kv_ref.at[from_level]
+        block_ref, block_sem = staging
+        copy = pltpu.make_async_copy(kv_ref.at[from_level], block_ref, block_sem)
+        copy.start()
+        copy.wait()
+        return block_ref
+
+    def query_fold(kv_ref, from_level, own):
+        block_ref = block_of(kv_ref, from_level)
+        if own:
+            key_mask = None
+        else:
+            mask_rows = block_ref[rows:, :].astype(jnp.float32)
+            key_mask = jnp.concatenate(
+                [mask_rows[0:1, : rows // 2], mask_rows[1:2, : rows // 2]], axis=1
             )
-            return (new_max, new_sum, new_acc)
-
-        return (lax.cond(key_pos[0] <= own_pos[-1], one_compute, keep_state, running), None)
-
-    blocks = (
-        split_blocks(key_part, blk_rows),
-        split_blocks(val_part, blk_rows),
-        split_blocks(doc_part, blk_rows),
-        jnp.arange(blk_count, dtype=jnp.int32),
-    )
-    result, unused = lax.scan(one_block, fold_state, blocks)
-    return result
+
+        def part(index, unused):
+            here = pl.ds(pl.multiple_of(index * chunk, chunk), chunk)
+            query = query_col_ref[level, here, :]
+            grad = grad_ref[here, :]
+            keys = block_ref[:rows, :width]
+            vals = block_ref[:rows, width:]
+            if own:
+                q_pos = index * chunk + lax.broadcasted_iota(jnp.int32, (chunk, rows), 0)
+                k_pos = lax.broadcasted_iota(jnp.int32, (chunk, rows), 1)
+                visible = (q_pos >= k_pos) & (doc_col_ref[here, :] == doc_row_ref[0:1, :])
+            products = []
+            for head in range(heads):
+                scores = dot_rows(query * head_mask[head], keys)
+                if own:
+                    scores = jnp.where(visible, scores, NEGATIVE)
+                    lse = stat_ref[head, here, :]
+                else:
+                    scores = scores + key_mask
+                    lse = stat_ref[heads + head, here, :]
+                probs = jnp.exp(scores - lse)
+                pull = dot_rows(grad * head_mask[head], vals) - stat_ref[2 * heads + head, here, :]
+                products.append(dot_plain((probs * pull).astype(jnp.bfloat16), keys))
+            dq_ref[here, :] = dq_ref[here, :] + pick_heads(products, lane_head)
+            return unused
+
+        lax.fori_loop(0, rows // chunk, part, 0)
+
+    query_fold(kv_col_ref, level, True)
+
+    @pl.when(side == 1)
+    def _():
+        query_fold(kv_oth_ref, level, False)
+
+    def earlier(from_level, unused):
+        query_fold(kv_col_ref, from_level, False)
+        query_fold(kv_oth_ref, from_level, False)
+        return unused
+
+    lax.fori_loop(0, level, earlier, 0)
+    dq_ref[...] = dq_ref[...] * (DH**-0.5)
+
+    own_block_ref = block_of(kv_col_ref, level)
+
+    def key_fold(query_ref, grads_ref, from_level, own):
+        def part(index, unused):
+            here = pl.ds(pl.multiple_of(index * chunk, chunk), chunk)
+            keys = own_block_ref[here, :width]
+            vals = own_block_ref[here, width:]
+            if own:
+                query = query_col_ref[level]
+                extended = own_ref[...]
+                k_pos = index * chunk + lax.broadcasted_iota(jnp.int32, (chunk, rows), 0)
+                q_pos = lax.broadcasted_iota(jnp.int32, (chunk, rows), 1)
+                visible = (q_pos >= k_pos) & (doc_col_ref[here, :] == doc_row_ref[0:1, :])
+            else:
+                query = query_ref[from_level]
+                extended = grads_ref[from_level]
+            grad = extended[:, :width]
+            stats = stat_rows(extended, width, 8)
+            key_parts, val_parts = [], []
+            for head in range(heads):
+                scores = dot_rows(keys * head_mask[head], query)
+                if own:
+                    scores = jnp.where(visible, scores, NEGATIVE)
+                probs = jnp.exp(scores - stats[head : head + 1, :])
+                val_parts.append(dot_plain(probs.astype(jnp.bfloat16), grad))
+                pull = dot_rows(vals * head_mask[head], grad) - stats[heads + head : heads + head + 1, :]
+                key_parts.append(dot_plain((probs * pull).astype(jnp.bfloat16), query))
+            dk_ref[here, :] = dk_ref[here, :] + pick_heads(key_parts, lane_head)
+            dv_ref[here, :] = dv_ref[here, :] + pick_heads(val_parts, lane_head)
+            return unused
+
+        lax.fori_loop(0, rows // chunk, part, 0)
+
+    @pl.when(side == 0)
+    def _():
+        oth_copy(level).wait_recv()
+        key_fold(query_oth_ref, grad_oth_ref, level, False)
+
+    def later(step, unused):
+        from_level = level + step
+        col_copy(from_level, level).wait_recv()
+        oth_copy(from_level).start()
+        key_fold(query_col_ref, grad_col_ref, from_level, False)
+        oth_copy(from_level).wait_recv()
+        key_fold(query_oth_ref, grad_oth_ref, from_level, False)
+        return unused
+
+    lax.fori_loop(1, levels - level, later, 0)
+    reaches = doc_col_ref[...] >= (seq + 1) * rows
+    dk_ref[...] = jnp.where(reaches, dk_ref[...], 0.0)
+    dv_ref[...] = jnp.where(reaches, dv_ref[...], 0.0)
+    key_fold(None, None, level, True)
+
+    @pl.when(side == 1)
+    def _():
+        oth_copy(level).wait_send()
+
+    def sent_down(step, unused):
+        col_copy(level, level - step).wait_send()
+        return unused
+
+    lax.fori_loop(1, level + 1, sent_down, 0)
+
+    def sent_on(step, unused):
+        oth_copy(level + step).wait_send()
+        return unused
+
+    lax.fori_loop(1, levels - level, sent_on, 0)
+
+
+def attention_backward(levels, grad, attended, lse, query_col, query_oth, kv_col, kv_oth, doc_ids):
+    rows, width = grad.shape
+    heads = width // DH
+    vmem = pl.BlockSpec(memory_space=pltpu.VMEM)
+    dma = pltpu.SemaphoreType.DMA
+    full = jax.ShapeDtypeStruct((rows, width), jnp.float32)
+    staged = levels > 8
+    far = pl.BlockSpec(memory_space=pl.ANY) if staged else vmem
+    staging = [pltpu.VMEM(kv_col.shape[1:], kv_col.dtype), dma(())] if staged else []
+    return pl.pallas_call(
+        functools.partial(backward_kernel, levels),
+        out_shape=(full, full, full),
+        in_specs=[vmem] * 5 + [far] * 2 + [vmem] * 2,
+        out_specs=(vmem,) * 3,
+        scratch_shapes=[
+            pltpu.VMEM((rows, LANES_OUT), jnp.bfloat16),
+            pltpu.VMEM((levels, rows, LANES_OUT), jnp.bfloat16),
+            pltpu.VMEM((levels, rows, LANES_OUT), jnp.bfloat16),
+            pltpu.VMEM((3 * heads, rows, 1), jnp.float32),
+            dma((levels,)),
+            dma((levels,)),
+            dma((levels,)),
+            dma((levels,)),
+            *staging,
+        ],
+        name="attention_backward",
+        compiler_params=pltpu.CompilerParams(
+            collective_id=2, has_side_effects=True, vmem_limit_bytes=VMEM_LIMIT
+        ),
+    )(grad, attended, lse, query_col, query_oth, kv_col, kv_oth, doc_ids[:, None], doc_ids[None, :])
 
 
 def local(
@@ -194,36 +731,27 @@
     key_mu = jnp.einsum("nhd,hn->hd", mem_keys.astype(jnp.float32), mu_weight, precision=UPPER_LIMIT) * scale_dh
     key_sigma = jnp.einsum("nhd,hn->hd", mem_keys.astype(jnp.float32), sigma_weight, precision=UPPER_LIMIT) * scale_dh
     hidden_in = tokens.astype(jnp.float32)
-    normed_one_f, norm_one_back = jax.vjp(layer_norm, hidden_in, ln1_gain, ln1_bias)
-    normed_one = normed_one_f.astype(jnp.bfloat16)
-    mixed_qkv = jnp.einsum(
-        "td,dcm->tcm", normed_one, qkv_weight, preferred_element_type=jnp.float32
-    )
-    queries = (mixed_qkv[:, 0] + qv_bias[0]).astype(jnp.bfloat16).reshape(head_shape)
-    key_rows = mixed_qkv[:, 1].astype(jnp.bfloat16).reshape(head_shape)
-    val_rows = (mixed_qkv[:, 2] + qv_bias[1]).astype(jnp.bfloat16).reshape(head_shape)
-    zero_heads = jnp.zeros(head_shape, jnp.float32)
-    fold_init = (
-        jnp.full((tok_rows, heads_here), NEGATIVE, jnp.float32),
-        jnp.zeros((tok_rows, heads_here), jnp.float32),
-        zero_heads,
-    )
-    row_max, row_sum, accumulated = forward_folder(
-        queries,
-        own_pos,
-        doc_ids,
-        scale_dh,
-        fold_init,
-        (
-            lax.all_gather(key_rows, "seq", axis=0, tiled=True),
-            lax.all_gather(val_rows, "seq", axis=0, tiled=True),
-            lax.all_gather(doc_ids, "seq", axis=0, tiled=True),
-        ),
-    )
-    log_sum = row_max + jnp.log(row_sum)
-    local_out = accumulated / row_sum[..., None]
+    unused, norm_one_back = jax.vjp(layer_norm, hidden_in, ln1_gain, ln1_bias)
+    levels = seq_count // 2
+    row_pad = ((0, 6), (0, 0))
+    norm_rows = jnp.pad(jnp.stack([ln1_gain, ln1_bias]), row_pad)
+    qkv_flat = qkv_weight.reshape(D, 3 * head_cols)
+    bias_row = jnp.concatenate([qv_bias[0], jnp.zeros(head_cols, jnp.float32), qv_bias[1]])
+    bias_rows = jnp.broadcast_to(bias_row[None], (8, 3 * head_cols))
+    reaches = doc_ids >= (seq_index + 1) * tok_rows
+    key_mask = jnp.where(reaches, 0.0, NEGATIVE).astype(jnp.bfloat16).reshape(2, tok_rows // 2)
+    key_mask = jnp.pad(key_mask, ((0, 14), (0, 2 * head_cols - tok_rows // 2)))
+    normed_one, query_col, kv_col, local_flat, log_sum = attention_forward(
+        levels, tokens, norm_rows, qkv_flat, bias_rows, doc_ids, key_mask
+    )
+    swap = [(index, index ^ 1) for index in range(seq_count)]
+    query_oth = lax.ppermute(query_col, "seq", swap)
+    kv_oth = lax.ppermute(kv_col, "seq", swap)
+    queries = lax.dynamic_index_in_dim(query_col, seq_index // 2, 0, False)
+    queries = (queries.astype(jnp.float32) / scale_dh).reshape(head_shape)
+    local_out = local_flat.reshape(head_shape)
     rbf_width = 1.0 / NB
-    queries_f = queries.astype(jnp.float32)
+    queries_f = queries
     centre = jax.nn.sigmoid(jnp.sum(queries_f * key_mu, axis=-1))
     loose = jnp.sum(queries_f * key_sigma, axis=-1)
     spread_sq = SPREAD * jax.nn.softplus(loose) + rbf_width * rbf_width
@@ -309,67 +837,20 @@
     grad_mem_seg = jnp.concatenate(
         [grad_mem_keys.reshape(NB, head_cols), grad_mem_vals.reshape(NB, head_cols)], axis=-1
     ).astype(jnp.bfloat16)
-    row_delta = jnp.sum(grad_heads.astype(jnp.float32) * local_out, axis=-1)
-
-    def cycle_step(step, carry):
-        key_blk, val_blk, doc_blk, grad_k, grad_v, grad_q = carry
-        anchor = (seq_index - step) % seq_count
-        key_pos = anchor * tok_rows + jnp.arange(tok_rows, dtype=jnp.int32)
-
-        def cycle_compute(current):
-            acc_k, acc_v, acc_q = current
-            visible = (
-                (own_pos[:, None] >= key_pos[None, :]) & (doc_ids[:, None] == doc_blk[None, :])
-            )[:, None, :]
-            scores = (
-                jnp.einsum("qhd,khd->qhk", queries, key_blk, preferred_element_type=jnp.float32)
-                * scale_dh
-            )
-            prob_vals = jnp.where(
-                visible, jnp.exp(jnp.where(visible, scores, NEGATIVE) - log_sum[..., None]), 0.0
-            )
-            acc_v = acc_v + jnp.einsum(
-                "qhk,qhd->khd",
-                prob_vals.astype(jnp.bfloat16),
-                grad_heads,
-                preferred_element_type=jnp.float32,
-            )
-            grad_prob = jnp.einsum(
-                "qhd,khd->qhk", grad_heads, val_blk, preferred_element_type=jnp.float32
-            )
-            grad_score = (prob_vals * (grad_prob - row_delta[..., None])).astype(jnp.bfloat16)
-            acc_q = (
-                acc_q
-                + jnp.einsum(
-                    "qhk,khd->qhd", grad_score, key_blk, preferred_element_type=jnp.float32
-                )
-                * scale_dh
-            )
-            acc_k = (
-                acc_k
-                + jnp.einsum(
-                    "qhk,qhd->khd", grad_score, queries, preferred_element_type=jnp.float32
-                )
-                * scale_dh
-            )
-            return (acc_k, acc_v, acc_q)
-
-        grad_k, grad_v, grad_q = lax.cond(
-            anchor <= seq_index, cycle_compute, keep_state, (grad_k, grad_v, grad_q)
-        )
-        key_blk, val_blk, doc_blk = shifted((key_blk, val_blk, doc_blk), "seq", 1)
-        grad_k, grad_v = (
-            passed_along(grad_k.astype(jnp.bfloat16), "seq", 1).astype(grad_k.dtype),
-            passed_along(grad_v.astype(jnp.bfloat16), "seq", 1).astype(grad_v.dtype),
-        )
-        return (key_blk, val_blk, doc_blk, grad_k, grad_v, grad_q)
-
-    cycle_init = (key_rows, val_rows, doc_ids, zero_heads, zero_heads, zero_heads)
-    cycle_final = lax.fori_loop(0, seq_count, cycle_step, cycle_init)
-    grad_keys, grad_vals, grad_q_local = (cycle_final[3], cycle_final[4], cycle_final[5])
-    grad_q_bf = (grad_q_local + grad_q_mem).astype(jnp.bfloat16).reshape(tok_rows, head_cols)
-    grad_k_bf = grad_keys.astype(jnp.bfloat16).reshape(tok_rows, head_cols)
-    grad_v_bf = grad_vals.astype(jnp.bfloat16).reshape(tok_rows, head_cols)
+    grad_q_local, grad_keys, grad_vals = attention_backward(
+        levels,
+        grad_heads.reshape(tok_rows, head_cols),
+        local_flat,
+        log_sum,
+        query_col,
+        query_oth,
+        kv_col,
+        kv_oth,
+        doc_ids,
+    )
+    grad_q_bf = (grad_q_local + grad_q_mem.reshape(tok_rows, head_cols)).astype(jnp.bfloat16)
+    grad_k_bf = grad_keys.astype(jnp.bfloat16)
+    grad_v_bf = grad_vals.astype(jnp.bfloat16)
     grad_qkv = jnp.stack([grad_q_bf, grad_k_bf, grad_v_bf], axis=1)
     grad_qkv_w = jnp.einsum("td,tcm->dcm", normed_one, grad_qkv, preferred_element_type=jnp.float32)
     grad_kv_w = jnp.einsum("nd,nm->dm", coeffs, grad_mem_seg, preferred_element_type=jnp.float32)

time: 801 us -> 599 us (0.75)
  starting transfers between devices: 146 us -> 2.79 us
  waiting for transfers between devices: 349 us -> 218 us
  Pallas kernels: 0 us -> 92 us
  blocking collectives: 96.1 us -> 135 us
  other arithmetic: 64.9 us -> 36.9 us
  loops' own time: 17 us -> 0 us
  local copies, waits for them, and re-layouts: 65.5 us -> 49.2 us
    ppermute x40 -> x2, starting transfers between devices: 144 us -> 2.03 us  [the longest x1 1.52 us: local(): query_oth = lax.ppermute(query_col, 'seq', swap)]
    pallas_call x0 -> x2, Pallas kernels: none -> 92 us  [the longest x1 51.1 us: attention_backward(): pl.pallas_call(functools.partial(backward_kernel, levels), out_shape=(ful...]
    all_gather x2 -> x0, waiting for transfers between devices: 69.1 us -> none  [the longest x1 38.8 us: local(): lax.all_gather(key_rows, 'seq', axis=0, tiled=True)]
    all_gather x1, blocking collectives: 22.2 us -> 86.5 us  [local(): lax.all_gather(jnp.stack([past_book, past_age]), 'seq', axis=1, tiled=True)]
    psum x1, waiting for transfers between devices: 71.7 us -> 24.5 us  [local(): lax.psum(jnp.dot(heads_out, out_weight, preferred_element_type=jnp.float3...]
    all_gather x1 -> x0, blocking collectives: 26.3 us -> none  [local(): lax.all_gather(doc_ids, 'seq', axis=0, tiled=True)]
    convert_element_type x34 -> x2, other arithmetic: 20.3 us -> 1.67 us  [the longest x1 0.98 us: local(): queries = (queries.astype(jnp.float32) / scale_dh).reshape(head_shape)]
    another operation x18 -> x0, loops' own time: 17 us -> none  [the longest x1 15.9 us: forward_folder(): result, unused = lax.scan(one_block, fold_state, blocks)]
  transfers between devices with their start and end apart: 50 -> 10, of which waited for: 13 -> 6; matrix products, arithmetic and copies ran while one was open for 15% -> 20% of each run, Pallas kernels for 0% -> 16%
where the time goes in v2:
time: 599 us; the launch traced here: 590 us
  waiting for transfers between devices  218 us (36%)
  blocking collectives  135 us (23%)
  Pallas kernels  92 us (15%)
  local copies, waits for them, and re-layouts  49.2 us (8%)
  matrix products  38.8 us (6%)
  other arithmetic  36.9 us (6%)
  between operations  17.4 us (3%)
    all_gather x1, blocking collectives, local(): lax.all_gather(jnp.stack([past_book, past_age]), 'seq', axis=1, tiled=True)  86.5 us
    reduce_scatter x1, waiting for transfers between devices, local(): lax.psum_scatter(grad_proj_w.astype(jnp.bfloat16), 'seq', scatter_dimensi...  65.2 us
    reduce_scatter x1, waiting for transfers between devices, local(): lax.psum_scatter(grad_fc_w.astype(jnp.bfloat16), 'seq', scatter_dimension...  64.9 us
    pallas_call x1, Pallas kernels, attention_backward(): pl.pallas_call(functools.partial(backward_kernel, levels), out_shape=(ful...  51.1 us
    pallas_call x1, Pallas kernels, attention_forward(): pl.pallas_call(functools.partial(forward_kernel, levels), out_shape=(jax....  40.9 us
    psum x1, blocking collectives, local(): lax.psum((grad_ln1_g, grad_ln1_b, grad_qv_b, grad_out_b, grad_ln2_g, grad...  39.1 us
    psum x1, waiting for transfers between devices, local(): lax.psum(jnp.einsum('tf,df->td', pre_bf, fc_weight, preferred_element_typ...  27.1 us
    psum x1, waiting for transfers between devices, local(): lax.psum(jnp.dot(heads_out, out_weight, preferred_element_type=jnp.float3...  24.5 us
  transfers between devices with their start and end apart: 10, of which 6 were waited for; matrix products, arithmetic and copies ran while one was open for 20% of the time, Pallas kernels for 16%

profile of v2, /device:TPU:0, one launch (start us, length us, event | category | flops | bytes accessed | tf_op | source)
XLA Modules:
  0.0 589.6 jit_solution(10033887523877347925)
XLA Ops:
  7.3 2.0 constant_dynamic-slice_fusion
  11.4 1.5 copy.97.doc_col_ref
  16.2 40.9 %attention_forward.1 = (bf16[512,768]{1,0:T(8,128)(2,1)}, bf16[4,512,192]{2,1,0:T(8,128)(2,1)}, bf16[4,528,384]{2,1,0:T(8,128)(2,1)}, f32[512,192]{1,0:T(8,128)}, f32[512,8]{1,0:T(8,128)}) custom-call(bf16[512,768]{1,0:T(8,128)(2,1)} %tok_ref.1, f32[8,768]{1,0:T(8,128)} %select_maximum_fusion.norm_ref, bf16[768,576]{1,0:T(8,128)(2,1)} %copy.96.weight_ref, ...), custom_call_target="tpu_custom_call" | custom-call | tf_op jit(solution)/shard_map/attention_forward/pallas_call | solution.py:383
  57.1 2.2 copy.105
  59.4 1.5 collective-permute-start
  62.8 86.5 %all-gather.1 = s32[8,1,2]{2,1,0:T(1,128)S(1)} all-gather(s32[1,1,2]{2,1,0:T(1,128)S(1)} %add_bitcast_fusion), channel_id=1, replica_groups=mesh['seq'=8,'tp'=4] {'seq'}, dimensions={0}, use_global_device_ids=true | all-gather | bytes 72 | tf_op jit(solution)/shard_map/all_gather | solution.py:705
  152.9 3.1 copy.128
  158.3 9.0 %all_gather.15 = bf16[512,768]{0,1:T(8,128)(2,1)S(1)} all-gather(bf16[512,192]{0,1:T(8,128)(2,1)S(1)} %fusion.46), channel_id=1, replica_groups=mesh['seq'=8,'tp'=4] {'tp'}, dimensions={1}, use_global_device_ids=true | all-gather | bytes 983040 | tf_op jit(solution)/shard_map/all_gather | solution.py:720
  171.8 3.3 fusion.84
  175.1 2.3 copy.107.query_oth_ref
  178.0 24.5 %all-reduce.8.cloned.1.call-done = bf16[512,768]{1,0:T(8,128)(2,1)} async-done(((bf16[512,768]{1,0:T(8,128)(2,1)}), bf16[512,768]{1,0:T(8,128)(2,1)}) %all-reduce.8.cloned.1.call-update) | async-done | bytes 786448 | tf_op jit(solution)/shard_map/psum | solution.py:769
  202.5 1.6 fusion.33
  205.2 3.7 convert_reduce_fusion.4
  209.8 1.7 convolution_convert_fusion.2
  215.5 3.8 convolution_convert_fusion.3
  219.3 27.1 %all-reduce.10.cloned.1.call-done = bf16[512,768]{1,0:T(8,128)(2,1)} async-done(((bf16[512,768]{1,0:T(8,128)(2,1)}), bf16[512,768]{1,0:T(8,128)(2,1)}) %all-reduce.10.cloned.1.call-update) | async-done | bytes 786448 | tf_op jit(solution)/shard_map/psum | solution.py:798
  246.3 2.7 convert_reduce_fusion.1
  249.1 1.6 fusion.23
  250.7 1.4 convert_reduce_fusion.5
  254.1 1.9 copy.131
  256.1 2.3 convolution_convert_fusion.9
  258.3 1.8 copy.106.grad_ref
  260.1 2.8 fusion.5
  264.3 2.0 copy.110
  266.3 2.0 copy.114
  269.1 2.0 copy.109
  271.1 2.0 copy.113
  274.6 51.1 %attention_backward.1 = (f32[512,192]{1,0:T(8,128)}, f32[512,192]{1,0:T(8,128)}, f32[512,192]{1,0:T(8,128)}) custom-call(bf16[512,192]{1,0:T(8,128)(2,1)} %copy.106.grad_ref, f32[512,192]{1,0:T(8,128)} %get-tuple-element.36.attended_ref, f32[512,8]{1,0:T(8,128)} %get-tuple-element.38.lse_ref, bf16[4,512,192]{2,1,0:T(8,128)(2,1)} %get-tuple-element.37.query_col_ref, ...), custom_call_target="tpu_custom_call" | custom-call | tf_op jit(solution)/shard_map/attention_backward/pallas_call | solution.py:645
  327.0 1.8 convert_reduce_fusion.6
  330.1 1.7 bitcast_convert_fusion
  331.9 2.2 pad_maximum_fusion
  334.0 2.2 copy.112
  336.3 2.7 fusion.43
  343.6 2.3 copy.129
  346.0 3.2 convolution_convert_fusion.1
  349.3 3.5 convolution_convert_fusion
  361.4 1.5 copy.132
  362.9 1.4 convert_element_type.189
  364.3 16.1 %all-reduce.12.cloned.1.call-done = (bf16[512,768]{1,0:T(8,128)(2,1)}, bf16[512,768]{1,0:T(8,128)(2,1)}) async-done(((bf16[512,768]{1,0:T(8,128)(2,1)}, bf16[512,768]{1,0:T(8,128)(2,1)}), (bf16[512,768]{1,0:T(8,128)(2,1)}, bf16[512,768]{1,0:T(8,128)(2,1)})) %all-reduce.12.cloned.1.call-update) | async-done | bytes 1572880 | tf_op jit(solution)/shard_map/psum | solution.py:782
  380.5 2.6 fusion.21
  383.1 1.5 fusion.24
  384.6 3.2 add_convert_fusion
  387.8 39.1 %all-reduce.2 = (f32[2,192]{1,0:T(2,128)}, f32[768]{0:T(1024)}, f32[768]{0:T(1024)}, f32[768]{0:T(1024)}, f32[768]{0:T(1024)}, /*index=5*/f32[768]{0:T(1024)}, f...) all-reduce(f32[2,192]{1,0:T(2,128)} %pad_maximum_fusion.2, ...), channel_id=1, replica_groups=mesh['seq'=8,'tp'=4] {'seq'}, use_global_device_ids=true, to_apply=%region_22.23 | all-reduce | flops 8832 | bytes 70656 | tf_op jit(solution)/shard_map/psum | solution.py:884
  426.9 20.1 %reduce-scatter.13.cloned.1.call-done = bf16[96,576]{1,0:T(8,128)(2,1)} async-done(((bf16[768,576]{1,0:T(8,128)(2,1)}), bf16[96,576]{1,0:T(8,128)(2,1)}) %reduce-scatter.13.cloned.1.call-update) | async-done | bytes 110608
  449.0 64.9 %reduce-scatter.9.cloned.1.call-done = bf16[96,768]{1,0:T(8,128)(2,1)} async-done(((bf16[768,768]{1,0:T(8,128)(2,1)}), bf16[96,768]{1,0:T(8,128)(2,1)}) %reduce-scatter.9.cloned.1.call-update) | async-done | bytes 147472 | tf_op jit(solution)/shard_map/reduce_scatter | solution.py:875
  513.9 1.6 convert_element_type.192
  515.5 65.2 %reduce-scatter.11.cloned.1.call-done = bf16[768,96]{0,1:T(8,128)(2,1)} async-done(((bf16[768,768]{0,1:T(8,128)(2,1)}), bf16[768,96]{0,1:T(8,128)(2,1)}) %reduce-scatter.11.cloned.1.call-update) | async-done | bytes 147472 | tf_op jit(solution)/shard_map/reduce_scatter | solution.py:876
  580.7 1.6 convert_element_type.195
  (224 shorter events, 45.6 us)
Async XLA Ops:
  7.2 198.0 %copy-start = (bf16[768,768]{1,0:T(8,128)(2,1)S(1)}, bf16[768,768]{1,0:T(8,128)(2,1)}, u32[]{:S(2)}) copy-start(bf16[768,768]{1,0:T(8,128)(2,1)} %param.40) | copy-start | bytes 3538948
  7.2 5.8 copy-start.10
  7.2 7.7 %copy-start.62 = (f32[2,192]{1,0:T(2,128)S(1)}, f32[2,192]{1,0:T(2,128)}, u32[]{:S(2)}) copy-start(f32[2,192]{1,0:T(2,128)} %param.35) | copy-start | bytes 4612
  7.2 145.7 %all-gather.4.cloned.1.call-start = ((), (), s32[]{:S(2)}) async-start(), calls=%async_computation.8 | async-start | bytes 2359296 | tf_op jit(solution)/shard_map/all_gather | solution.py:704
  9.3 193.2 %all-reduce.8.cloned.1.call-start = ((), (), s32[]{:S(2)}) async-start(), calls=%async_computation.4 | async-start | bytes 1572864 | tf_op jit(solution)/shard_map/psum | solution.py:769
  57.1 92.9 %copy-start.14 = (f32[512,192]{1,0:T(8,128)S(1)}, f32[512,192]{1,0:T(8,128)}, u32[]{:S(2)}) copy-start(f32[512,192]{1,0:T(8,128)} %get-tuple-element.36.attended_ref) | copy-start | bytes 1179652
  59.4 115.7 %collective-permute-start = (bf16[4,512,192]{1,2,0:T(8,128)(2,1)}, bf16[4,512,192]{1,2,0:T(8,128)(2,1)}, u32[]{:S(2)}, u32[]{:S(2)}) collective-permute-start(bf16[4,512,192]{1,2,0:T(8,128)(2,1)} %copy.105), channel_id=1, source_target_pairs={{0,4},{4,0},{8,12},{12,8},{16,20},{20,16},{24,28},{28,24},{1,5},{5... | collective-permute-start | bytes 2359304 | tf_op jit(solution)/shard_map/ppermute | solution.py:748
  62.3 212.3 %collective-permute-start.1 = (bf16[4,528,384]{2,1,0:T(8,128)(2,1)}, bf16[4,528,384]{2,1,0:T(8,128)(2,1)}, u32[]{:S(2)}, u32[]{:S(2)}) collective-permute-start(bf16[4,528,384]{2,1,0:T(8,128)(2,1)} %get-tuple-element.39.kv_col_ref), channel_id=1, source_target_pairs={{0,4},{4,0},{8,12},{12,8},{16,20},{20,16},{24,28},{28,24},{1,5},{5... | collective-permute-start | bytes 4866056 | tf_op jit(solution)/shard_map/ppermute | solution.py:749
  152.8 16.3 %copy-start.63 = (f32[512]{0:T(512)}, f32[512]{0:T(512)S(1)}, u32[]{:S(2)}) copy-start(f32[512]{0:T(512)S(1)} %add_multiply_fusion) | copy-start | bytes 6148
  157.7 9.5 %copy-start.11 = (bf16[768,3,192]{0,2,1:T(8,128)(2,1)S(1)}, bf16[768,3,192]{0,2,1:T(8,128)(2,1)}, u32[]{:S(2)}) copy-start(bf16[768,3,192]{0,2,1:T(8,128)(2,1)} %param.34) | copy-start | bytes 2654212
  158.3 9.7 %copy-start.56 = (f32[3,512]{1,0:T(4,128)S(1)}, f32[3,512]{1,0:T(4,128)}, u32[]{:S(2)}) copy-start(f32[3,512]{1,0:T(4,128)} %param.44) | copy-start | bytes 18436
  170.2 4.9 copy-start.25
  171.6 74.7 %all-reduce.10.cloned.1.call-start = ((), (), s32[]{:S(2)}) async-start(), calls=%async_computation.5 | async-start | bytes 1572864 | tf_op jit(solution)/shard_map/psum | solution.py:798
  175.1 27.4 %copy-start.1 = (bf16[512,768]{1,0:T(8,128)(2,1)S(1)}, bf16[512,768]{1,0:T(8,128)(2,1)}, u32[]{:S(2)}) copy-start(bf16[512,768]{1,0:T(8,128)(2,1)} %tok_ref.1) | copy-start | bytes 2359300
  175.1 27.4 %copy-start.32 = (f32[768]{0:T(1024)S(1)}, f32[768]{0:T(1024)}, u32[]{:S(2)}) copy-start(f32[768]{0:T(1024)} %param.37) | copy-start | bytes 9220
  202.5 2.7 copy-start.35
  202.5 2.7 copy-start.64
  202.5 2.7 copy-start.65
  202.5 2.7 copy-start.66
  205.2 3.7 copy-start.41
  211.5 149.9 %reduce-scatter.15.cloned.1.call-start = ((), (), s32[]{:S(2)}) async-start(), calls=%async_computation.10 | async-start | bytes 442368
  246.3 2.7 copy-start.50
  246.3 2.7 copy-start.3
  246.3 2.7 copy-start.36
  246.3 2.7 copy-start.42
  249.1 3.1 copy-start.39
  256.0 124.4 %all-reduce.12.cloned.1.call-start = ((), (), s32[]{:S(2)}) async-start(), calls=%async_computation.11 | async-start | bytes 3145728 | tf_op jit(solution)/shard_map/psum | solution.py:782
  260.1 2.8 copy-start.34
  263.5 4.8 copy-start.46
  274.6 64.7 %copy-start.51 = (f32[192]{0:T(256)}, f32[192]{0:T(256)S(1)}, u32[]{:S(2)}) copy-start(f32[192]{0:T(256)S(1)} %broadcast_multiply_fusion.5) | copy-start | bytes 2308
  274.6 64.7 %copy-start.52 = (f32[192]{0:T(256)}, f32[192]{0:T(256)S(1)}, u32[]{:S(2)}) copy-start(f32[192]{0:T(256)S(1)} %broadcast_multiply_fusion.4) | copy-start | bytes 2308
  325.7 3.1 copy-start.15
  325.7 3.1 copy-start.16
  325.7 3.0 copy-start.29
  325.7 3.0 copy-start.59
  325.7 3.0 copy-start.60
  325.7 4.4 copy-start.12
  339.0 108.1 %reduce-scatter.13.cloned.1.call-start = ((), (), s32[]{:S(2)}) async-start(), calls=%async_computation.9 | async-start | bytes 1105920
  345.9 3.4 copy-start.9
  345.9 168.0 %reduce-scatter.9.cloned.1.call-start = ((), (), s32[]{:S(2)}) async-start(), calls=%async_computation.6 | async-start | bytes 1327104 | tf_op jit(solution)/shard_map/reduce_scatter | solution.py:875
  349.2 231.4 %reduce-scatter.11.cloned.1.call-start = ((), (), s32[]{:S(2)}) async-start(), calls=%async_computation.7 | async-start | bytes 1327104 | tf_op jit(solution)/shard_map/reduce_scatter | solution.py:876
  352.8 27.6 %copy-start.38 = (f32[768]{0:T(1024)S(1)}, f32[768]{0:T(1024)}, u32[]{:S(2)}) copy-start(f32[768]{0:T(1024)} %param.32) | copy-start | bytes 9220
  380.4 4.2 copy-start.4
  380.4 4.2 copy-start.28
  380.4 4.1 copy-start.40
  380.4 4.1 copy-start.44
  380.5 4.1 copy-start.48
  380.5 4.1 copy-start.61
  (30 other events, 47.3 us)
Sparse Core Ops, SparseCore 0:
  10.8 71.0 all-gather.3
  171.7 30.7 all-reduce.7
  211.6 34.6 all-reduce.9
  256.1 61.5 reduce-scatter.14
  339.1 41.2 all-reduce.11
  383.6 63.4 reduce-scatter.12
  450.8 62.9 reduce-scatter.8
  517.6 62.9 reduce-scatter.10
